TPU v7x, 256 devices: a whole 4x4x8 slice. The times are simulated.
256 devices in a mesh: ctx: 32 (over z, x_hi, core), head: 8 (over y, x_lo).
Axes of the slice: x: 4 (x_hi: 2, x_lo: 2; x = x_hi * 2 + x_lo), y: 4, z: 8, core: 2. Of those that a mesh axis runs over, the one named last changes fastest.
Arguments:
- q_nope: bfloat16 [8192, 16384], P('ctx', 'head'), may hold values from -6 to 6
- q_rope: bfloat16 [8192, 8192], P('ctx', 'head'), may hold values from -48 to 48
- latent: bfloat16 [8192, 512], P(('ctx', 'head')), may hold values from -8 to 8
- amax_prior: float32 [512], replicated, may hold values from 0.5 to 4
- k_rope: bfloat16 [64, 8192], P(None, 'ctx'), may hold values from -6 to 6
- w_uk: bfloat16 [128, 128, 512], P('head'), may hold values from -0.5 to 0.5
- w_uv: bfloat16 [128, 512, 128], P('head'), may hold values from -0.25 to 0.25
- seg_ids: int32 [8192], P('ctx'), may hold values from 0 to 63, never falling along the last dimension, each value on 1 to 768 neighbouring positions
Outputs:
- attended: bfloat16 [8192, 16384], P('ctx', 'head')
- latent_amax: float32 [512], replicated
Inputs may be any that keep to these rules, and one draw needn't show every extreme that they name: seg_ids never falls along the tokens; each document has 1 to 768 tokens and one has exactly 768.
All inputs are finite; a program needn't handle non-finite values.
Results may differ from a plain program's by a relative error of at most 0.012.
Values may be sent and summed in bfloat16 or wider, within the bound.
A program may use at most 64 MiB of HBM per device.

v0:
```python
import math

import jax
import jax.numpy as jnp
from jax import lax
from jax.sharding import PartitionSpec as P


def entering(x, axis, combine, identity):
    peers, index = (lax.axis_size(axis), lax.axis_index(axis))
    everything = lax.all_gather(x, axis)
    start = jnp.broadcast_to(jnp.asarray(identity, x.dtype), x.shape)

    def lap(k, before):
        reached = k < index
        new = combine(before, everything[k])
        return jnp.where(reached, new, before)

    return lax.fori_loop(0, peers, lap, start)


def from_behind(block, axis, distance):
    devices = range(lax.axis_size(axis))
    route = [(i - distance, i) for i in devices if i - distance in devices]
    return lax.ppermute(block, axis, route)


def frequencies(rdim):
    return jnp.exp(jnp.arange(rdim // 2, dtype=jnp.float32) * (-2.0 * math.log(10000.0) / rdim))


def turn_rows(values, angle):
    half = values.shape[-1] // 2
    first = values[..., :half]
    second = values[..., half:]
    cosine = jnp.cos(angle)
    sine = jnp.sin(angle)
    return jnp.concatenate(
        [first * cosine - second * sine, second * cosine + first * sine], axis=-1
    )


def turn_cols(values, angle):
    half = values.shape[0] // 2
    first = values[:half]
    second = values[half:]
    cosine = jnp.cos(angle)
    sine = jnp.sin(angle)
    return jnp.concatenate([first * cosine - second * sine, second * cosine + first * sine], axis=0)


def add_counts(first, second):
    return first + second


def saturate(rows, amax_prior):
    return jnp.clip(rows.astype(jnp.float32) / amax_prior[None, :], -1.0, 1.0).astype(jnp.bfloat16)


def shards(q_nope, q_rope, latent, amax_prior, k_rope, w_uk, w_uv, seg_ids):
    tokens_here = q_nope.shape[0]
    heads_here = w_uk.shape[0]
    head_size = w_uk.shape[1]
    rope_width = k_rope.shape[0]
    nseg = 2 * lax.axis_size("ctx")
    block_index = lax.axis_index("ctx")
    onehot = (seg_ids[:, None] == jnp.arange(nseg, dtype=jnp.int32)[None, :]).astype(jnp.int32)
    counts = jnp.sum(onehot, axis=0)
    earlier = entering(counts, "ctx", add_counts, jnp.zeros_like(counts))
    local = jnp.arange(tokens_here, dtype=jnp.int32)
    preceding = jnp.sum((seg_ids[None, :] < seg_ids[:, None]).astype(jnp.int32), axis=1)
    positions = jnp.sum(onehot * earlier[None, :], axis=1) + local - preceding
    angle = positions.astype(jnp.float32)[:, None] * frequencies(rope_width)[None, :]
    k_turned = turn_cols(k_rope.astype(jnp.float32), angle.T).astype(jnp.bfloat16)
    q_turned = turn_rows(
        q_rope.reshape(tokens_here, heads_here, rope_width).astype(jnp.float32), angle[:, None, :]
    ).astype(jnp.bfloat16)
    latent_amax = lax.pmax(jnp.max(jnp.abs(latent.astype(jnp.float32)), axis=0), ("ctx", "head"))
    keys_here = lax.all_gather(saturate(latent, amax_prior), "head", axis=0, tiled=True)
    q_latent = jnp.einsum(
        "thd,hdc->thc",
        q_nope.reshape(tokens_here, heads_here, head_size),
        w_uk,
        preferred_element_type=jnp.float32,
    )
    q_absorbed = (q_latent * amax_prior[None, None, :]).astype(jnp.bfloat16)
    payload = (keys_here, k_turned)
    received = [payload]
    moving = payload
    for step in range(3):
        moving = from_behind((moving[0], moving[1]), "ctx", 1)
        received.append(moving)
    ordered = received[::-1]
    lat_all = jnp.concatenate([entry[0] for entry in ordered], axis=0)
    rope_all = jnp.concatenate([entry[1] for entry in ordered], axis=1)
    scale = (head_size + rope_width) ** (-0.5)
    scores = (
        jnp.einsum("thc,kc->thk", q_absorbed, lat_all, preferred_element_type=jnp.float32)
        + jnp.einsum("thr,rk->thk", q_turned, rope_all, preferred_element_type=jnp.float32)
    ) * scale
    q_index = block_index * tokens_here + local
    k_index = (block_index - 3) * tokens_here + jnp.arange(4 * tokens_here, dtype=jnp.int32)
    visible = (k_index[None, :] <= q_index[:, None]) & (
        k_index[None, :] >= (q_index - positions)[:, None]
    )
    scores = jnp.where(visible[:, None, :], scores, -1e30)
    top = jnp.max(scores, axis=-1, keepdims=True)
    exps = jnp.exp(scores - top)
    denom = jnp.sum(exps, axis=-1)
    weights = exps.astype(jnp.bfloat16)
    total = jnp.einsum("thk,kc->thc", weights, lat_all, preferred_element_type=jnp.float32)
    latent_out = (total * amax_prior[None, None, :] / denom[:, :, None]).astype(jnp.bfloat16)
    attended = jnp.einsum(
        "thc,hcd->thd", latent_out, w_uv, preferred_element_type=jnp.float32
    ).astype(jnp.bfloat16)
    return (attended.reshape(tokens_here, heads_here * head_size), latent_amax)


def solution(mesh):
    placed = (
        P("ctx", "head"),
        P("ctx", "head"),
        P(("ctx", "head"), None),
        P(),
        P(None, "ctx"),
        P("head", None, None),
        P("head", None, None),
        P("ctx"),
    )
    return jax.shard_map(
        shards, mesh=mesh, in_specs=placed, out_specs=(P("ctx", "head"), P()), check_vma=False
    )
```

profile of v0, /device:TPU:1, one launch (start us, length us, event | category | flops | bytes accessed | tf_op | source)
XLA Modules:
  0.0 206.9 jit_solution(15422379186148680088)
XLA Ops:
  0.6 0.0 copy-start
  0.7 0.9 convert_reduce_fusion.1
  1.6 0.9 convert_reduce_fusion
  2.6 1.3 dynamic-slice
  4.6 0.3 dynamic-update-slice
  4.9 18.7 %all-reduce = s32[2048]{0:T(1024)S(1)} all-reduce(s32[2048]{0:T(1024)S(1)} %dynamic-update-slice), channel_id=2, replica_groups=mesh['ctx'=32,'head'=8] {'ctx'}, use_global_device_ids=true, to_apply=%add | all-reduce | flops 2048 | bytes 16384
  23.6 0.1 reshape.150
  23.6 1.3 while.14
  24.9 0.8 select_reduce_fusion
  25.7 0.8 convert_element_type.58
  26.5 0.2 fusion.38
  26.7 0.6 pad_maximum_fusion
  27.3 7.8 %collective-permute-start.3 = (bf16[64,256]{1,0:T(8,128)(2,1)}, bf16[64,256]{1,0:T(8,128)(2,1)S(1)}, u32[]{:S(2)}, u32[]{:S(2)}) collective-permute-start(bf16[64,256]{1,0:T(8,128)(2,1)} %pad_maximum_fusion), channel_id=1, source_target_pairs={{0,8},{8,16},{16,24},{24,32},{32,40},{40,48},{48,56},{56,64},{64,7... | collective-permute-start | bytes 98312 | tf_op jit(solution)/shard_map/ppermute | solution.py:25
  35.1 0.8 fusion.32
  35.9 25.4 %all_gather.11 = bf16[256,512]{1,0:T(8,128)(2,1)} all-gather(bf16[32,512]{1,0:T(8,128)(2,1)S(1)} %get-tuple-element.114), channel_id=1, replica_groups=mesh['ctx'=32,'head'=8] {'head'}, dimensions={0}, use_global_device_ids=true | all-gather | bytes 294912 | tf_op jit(solution)/shard_map/all_gather | solution.py:79
  61.3 7.7 %collective-permute-start = (bf16[256,512]{1,0:T(8,128)(2,1)}, bf16[256,512]{1,0:T(8,128)(2,1)}, u32[]{:S(2)}, u32[]{:S(2)}) collective-permute-start(bf16[256,512]{1,0:T(8,128)(2,1)} %all_gather.11), channel_id=1, source_target_pairs={{0,8},{8,16},{16,24},{24,32},{32,40},{40,48},{48,56},{56,64},{64,7... | collective-permute-start | bytes 786440 | tf_op jit(solution)/shard_map/ppermute | solution.py:25
  69.0 0.2 multiply_cosine_fusion.1
  69.2 1.2 copy.13
  70.5 0.9 subtract_convert_fusion
  71.3 0.0 collective-permute-done.3
  71.3 1.9 collective-permute-start.4
  73.3 0.0 collective-permute-done
  73.3 5.2 %collective-permute-start.1 = (bf16[256,512]{1,0:T(8,128)(2,1)}, bf16[256,512]{1,0:T(8,128)(2,1)}, u32[]{:S(2)}, u32[]{:S(2)}) collective-permute-start(bf16[256,512]{1,0:T(8,128)(2,1)} %collective-permute-done), channel_id=1, source_target_pairs={{0,8},{8,16},{16,24},{24,32},{32,40},{40,48},{48,56},{56,64},{64,7... | collective-permute-start | bytes 786440 | tf_op jit(solution)/shard_map/ppermute | solution.py:25
  78.5 0.0 collective-permute-done.4
  78.6 1.9 collective-permute-start.5
  80.5 1.0 compare_and_fusion
  81.5 1.5 copy.18
  83.0 75.4 %pmax.7 = f32[512]{0:T(512)} all-reduce(f32[512]{0:T(512)S(1)} %get-tuple-element.113), channel_id=1, replica_groups=mesh['ctx'=32,'head'=8] {'ctx','head'}, use_global_device_ids=true, to_apply=%region_8.9 | all-reduce | flops 512 | bytes 4096 | tf_op jit(solution)/shard_map/pmax | solution.py:78
  158.3 0.0 collective-permute-done.1
  158.3 3.8 %collective-permute-start.2 = (bf16[256,512]{1,0:T(8,128)(2,1)}, bf16[256,512]{1,0:T(8,128)(2,1)S(1)}, u32[]{:S(2)}, u32[]{:S(2)}) collective-permute-start(bf16[256,512]{1,0:T(8,128)(2,1)} %collective-permute-done.1), channel_id=1, source_target_pairs={{0,8},{8,16},{16,24},{24,32},{32,40},{40,48},{48,56},{56,64},{64,7... | collective-permute-start | bytes 786440 | tf_op jit(solution)/shard_map/ppermute | solution.py:25
  162.1 0.0 collective-permute-done.5
  162.2 0.0 copy-start.1
  162.2 9.0 %fusion.18 = f32[256,16,1024]{2,0,1:T(8,128)} fusion(bf16[256,16,32]{0,2,1:T(8,128)(2,1)} %get-tuple-element.110, bf16[256,16,32]{0,2,1:T(8,128)(2,1)S(1)} %get-tuple-element.109, bf16[32,256]{1,0:T(8,128)(2,1)S(1)} %get-tuple-element.112, bf16[32,256]{1,0:T(8,128)(2,1)S(1)} %get-tuple-element.111, bf16[64,256]{1,0:T(8,128)(2,1)S(1)} %collective-permute-done.3, ...), kind=kOutput, calls=%fused_computation.17 | convolution fusion | flops 538574848 | bytes 17432576 | tf_op jit(solution)/shard_map/thr,rk->thk/dot_general | solution.py:99
  171.2 0.0 collective-permute-done.2
  171.2 0.0 copy-start.2
  171.2 0.7 copy-done.2
  171.9 0.0 copy-done
  171.9 0.0 copy-done.1
  171.9 14.5 %fusion.47 = (f32[256,16]{0,1:T(8,128)S(1)}, f32[256,16,1024]{2,0,1:T(8,128)}) fusion(f32[256,16,1024]{2,0,1:T(8,128)} %fusion.18, bf16[256,512]{1,0:T(8,128)(2,1)} %all_gather.11, bf16[256,512]{1,0:T(8,128)(2,1)} %collective-permute-done, bf16[256,512]{1,0:T(8,128)(2,1)} %collective-permute-done.1, bf16[256,512]{1,0:T(8,128)(2,1)} %copy-done.2, ...), kind=kOutput, calls=%fused_computation.63 | convolution fusion | flops 4856999936 | bytes 38029312 | tf_op jit(solution)/shard_map/thc,kc->thk/dot_general | solution.py:98
  186.4 7.7 %fusion = f32[256,16]{0,1:T(8,128)S(1)} fusion(f32[256,16,1024]{2,0,1:T(8,128)} %get-tuple-element.120, f32[256,16]{0,1:T(8,128)S(1)} %get-tuple-element.119), kind=kLoop, calls=%fused_computation.4 | loop fusion | flops 8384512 | bytes 16809984 | tf_op jit(solution)/shard_map/reduce_sum | solution.py:109
  194.1 11.3 %fusion.15 = bf16[16,256,128]{1,2,0:T(8,128)(2,1)S(1)} fusion(bf16[16,512,128]{2,1,0:T(8,128)(2,1)} %param.16, f32[256,16]{0,1:T(8,128)S(1)} %fusion, f32[512]{0:T(512)S(1)} %copy-done.1, f32[256,16,1024]{2,0,1:T(8,128)} %get-tuple-element.120, f32[256,16]{0,1:T(8,128)S(1)} %get-tuple-element.119, bf16[256,512]{1,0:T(8,128)(2,1)} %all_gather.11, ...), kind=kOutput, calls=%fused_computation.14 | convolution fusion | flops 4851236864 | bytes 21006336 | tf_op jit(solution)/shard_map/thc,hcd->thd/dot_general | solution.py:113
  205.5 1.4 copy.15
  (38 shorter events, 0.6 us)
Async XLA Ops:
  0.6 171.3 %copy-start = (bf16[16,128,512]{2,1,0:T(8,128)(2,1)S(1)}, bf16[16,128,512]{2,1,0:T(8,128)(2,1)}, u32[]{:S(2)}) copy-start(bf16[16,128,512]{2,1,0:T(8,128)(2,1)} %param.15) | copy-start | bytes 6291460
  27.3 44.1 %collective-permute-start.3 = (bf16[64,256]{1,0:T(8,128)(2,1)}, bf16[64,256]{1,0:T(8,128)(2,1)S(1)}, u32[]{:S(2)}, u32[]{:S(2)}) collective-permute-start(bf16[64,256]{1,0:T(8,128)(2,1)} %pad_maximum_fusion), channel_id=1, source_target_pairs={{0,8},{8,16},{16,24},{24,32},{32,40},{40,48},{48,56},{56,64},{64,7... | collective-permute-start | bytes 98312 | tf_op jit(solution)/shard_map/ppermute | solution.py:25
  61.3 12.0 %collective-permute-start = (bf16[256,512]{1,0:T(8,128)(2,1)}, bf16[256,512]{1,0:T(8,128)(2,1)}, u32[]{:S(2)}, u32[]{:S(2)}) collective-permute-start(bf16[256,512]{1,0:T(8,128)(2,1)} %all_gather.11), channel_id=1, source_target_pairs={{0,8},{8,16},{16,24},{24,32},{32,40},{40,48},{48,56},{56,64},{64,7... | collective-permute-start | bytes 786440 | tf_op jit(solution)/shard_map/ppermute | solution.py:25
  71.3 7.2 %collective-permute-start.4 = (bf16[64,256]{1,0:T(8,128)(2,1)S(1)}, bf16[64,256]{1,0:T(8,128)(2,1)S(1)}, u32[]{:S(2)}, u32[]{:S(2)}) collective-permute-start(bf16[64,256]{1,0:T(8,128)(2,1)S(1)} %collective-permute-done.3), channel_id=1, source_target_pairs={{0,8},{8,16},{16,24},{24,32},{32,40},{40,48},{48,56},{56,64},{64,7... | collective-permute-start | bytes 98312 | tf_op jit(solution)/shard_map/ppermute | solution.py:25
  73.3 85.1 %collective-permute-start.1 = (bf16[256,512]{1,0:T(8,128)(2,1)}, bf16[256,512]{1,0:T(8,128)(2,1)}, u32[]{:S(2)}, u32[]{:S(2)}) collective-permute-start(bf16[256,512]{1,0:T(8,128)(2,1)} %collective-permute-done), channel_id=1, source_target_pairs={{0,8},{8,16},{16,24},{24,32},{32,40},{40,48},{48,56},{56,64},{64,7... | collective-permute-start | bytes 786440 | tf_op jit(solution)/shard_map/ppermute | solution.py:25
  78.6 83.6 %collective-permute-start.5 = (bf16[64,256]{1,0:T(8,128)(2,1)S(1)}, bf16[64,256]{1,0:T(8,128)(2,1)S(1)}, u32[]{:S(2)}, u32[]{:S(2)}) collective-permute-start(bf16[64,256]{1,0:T(8,128)(2,1)S(1)} %collective-permute-done.4), channel_id=1, source_target_pairs={{0,8},{8,16},{16,24},{24,32},{32,40},{40,48},{48,56},{56,64},{64,7... | collective-permute-start | bytes 98312 | tf_op jit(solution)/shard_map/ppermute | solution.py:25
  158.3 12.9 %collective-permute-start.2 = (bf16[256,512]{1,0:T(8,128)(2,1)}, bf16[256,512]{1,0:T(8,128)(2,1)S(1)}, u32[]{:S(2)}, u32[]{:S(2)}) collective-permute-start(bf16[256,512]{1,0:T(8,128)(2,1)} %collective-permute-done.1), channel_id=1, source_target_pairs={{0,8},{8,16},{16,24},{24,32},{32,40},{40,48},{48,56},{56,64},{64,7... | collective-permute-start | bytes 786440 | tf_op jit(solution)/shard_map/ppermute | solution.py:25
  162.2 9.8 %copy-start.1 = (f32[512]{0:T(512)S(1)}, f32[512]{0:T(512)}, u32[]{:S(2)}) copy-start(f32[512]{0:T(512)} %param.13) | copy-start | bytes 6148
  171.2 0.7 copy-start.2
where the time goes:
time: 208 us; the launch traced here: 207 us
  blocking collectives  119 us (57%)
  matrix products  34.9 us (17%)
  starting transfers between devices  28.4 us (14%)
  other arithmetic  15.3 us (7%)
  local copies, waits for them, and re-layouts  6.56 us (3%)
    pmax x1, blocking collectives, shards(): lax.pmax(jnp.max(jnp.abs(latent.astype(jnp.float32)), axis=0), ('ctx', 'h...  75.4 us
    ppermute x6, starting transfers between devices, from_behind(): return lax.ppermute(block, axis, route)  28.4 us
    all_gather x1, blocking collectives, shards(): lax.all_gather(saturate(latent, amax_prior), 'head', axis=0, tiled=True)  25.4 us
    unnamed x1, blocking collectives  18.7 us
    dot_general x1, matrix products, shards(): jnp.einsum('thc,kc->thk', q_absorbed, lat_all, preferred_element_type=jnp...  14.5 us
    dot_general x1, matrix products, shards(): jnp.einsum('thc,hcd->thd', latent_out, w_uv, preferred_element_type=jnp.f...  11.3 us
    dot_general x1, matrix products, shards(): jnp.einsum('thr,rk->thk', q_turned, rope_all, preferred_element_type=jnp....  9.04 us
    reduce_sum x1, other arithmetic, shards(): denom = jnp.sum(exps, axis=-1)  7.69 us
  transfers between devices with their start and end apart: 6, of which 0 were waited for; matrix products, arithmetic and copies ran while one was open for 7% of the time, Pallas kernels for 0%

commit v1 on v0

v1 whole, which is shorter than its diff:
```python
import functools
import math

import jax
import jax.numpy as jnp
import numpy as np
from jax import lax
from jax.experimental import pallas as pl
from jax.experimental.pallas import tpu as pltpu
from jax.sharding import PartitionSpec as P

MESH = pl.DeviceIdType.MESH
BF16 = jnp.bfloat16
F32 = jnp.float32
BLOCKS = 4
HIDDEN = -1e30


def tables(tokens, rope, gain):
    half = rope // 2
    freq = np.exp(np.arange(half) * (-2.0 * math.log(10000.0) / rope))
    q_angle = np.arange(tokens)[:, None] * freq[None, :]
    q_cos = np.tile(np.cos(q_angle), (1, 4)).astype(np.float32)
    q_sin = np.tile(np.sin(q_angle), (1, 4)).astype(np.float32)
    k_place = np.arange(BLOCKS * tokens) - (BLOCKS - 1) * tokens
    k_angle = freq[:, None] * k_place[None, :]
    k_cos = (np.cos(k_angle) * gain).astype(np.float32)
    k_sin = (np.sin(k_angle) * gain).astype(np.float32)
    return q_cos, q_sin, k_cos, k_sin


def nt(a, b):
    return lax.dot_general(a, b, (((1,), (1,)), ((), ())), preferred_element_type=F32)


def nn(a, b):
    return jnp.dot(a, b, preferred_element_type=F32)


def kernel(
    n_ctx, n_head, gain,
    latent, prior, k_rope, seg, q_nope, q_rope, w_uk, w_uv, q_cos, q_sin, k_cos, k_sin,
    seen, qn, qx, kt, kx, vals, oldest, uk, uv, amax_out,
    lat, keys, tops, z_tops, prior_v, seg_v, qr, qc, qs, kc, ks, clipped,
    lat_recv, lat_send, ahead_send, keys_recv, keys_send, sib_send, sib_recv,
    tops_recv, tops_send, z_recv, z_send, load,
):
    ctx = lax.axis_index("ctx")
    me = lax.axis_index("head")
    core = lax.rem(ctx, 2)
    sibling = ctx + 1 - 2 * core
    n_z = n_ctx // 4
    z = ctx // 4
    heads, hd, width = uk.shape
    tokens = qn.shape[0]
    rope = k_rope.shape[0]
    rows = latent.shape[0]
    mine = pl.ds(pl.multiple_of(me * rows, rows), rows)

    kind = lax.rem(ctx, 4)
    has1 = ctx >= 2
    has2 = (core == 1) | (ctx >= 2)
    has0 = ctx >= 3
    next2 = ctx + 2 < n_ctx
    next3 = (core == 1) & (ctx + 3 < n_ctx)

    beside = me + 1 - 2 * lax.rem(me, 2)

    def along(h, d):
        return lax.rem(h + 2 * d + n_head, n_head)

    def rows_of(h):
        return pl.ds(pl.multiple_of(h * rows, rows), rows)

    def remote(src, dst, send, recv, c, h):
        return pltpu.make_async_remote_copy(
            src_ref=src, dst_ref=dst, send_sem=send, recv_sem=recv, device_id=(c, h), device_id_type=MESH
        )

    loads = [
        (latent, lat.at[3, mine]), (k_rope, keys.at[3, pl.ds(0, rope)]), (seg, seg_v), (prior, prior_v),
        (q_rope, qr), (q_cos, qc), (q_sin, qs), (k_cos, kc), (k_sin, ks), (w_uk, uk), (w_uv, uv), (q_nope, qn),
    ]
    loading = [pltpu.make_async_copy(src, dst, load.at[i]) for i, (src, dst) in enumerate(loads)]
    for copy in loading:
        copy.start()
    qn_load = loading[11]

    barrier = pltpu.get_barrier_semaphore()

    def greet(c, h):
        pl.semaphore_signal(barrier, inc=1, device_id=(c, h), device_id_type=MESH)

    for h in (beside, along(me, 1), along(me, -1)):
        greet(ctx, h)
    greet(sibling, me)
    for d in (1, 2, 3):
        greet(4 * z + lax.rem(kind + d, 4), me)
    for k in range(1, n_z):
        greet(4 * lax.rem(z + k, n_z) + kind, me)

    @pl.when(has1)
    def _():
        greet(ctx - 2, me)

    @pl.when((core == 0) & has0)
    def _():
        greet(ctx - 3, me)

    loading[0].wait()
    loading[1].wait()
    loading[2].wait()
    keys[3, rope:, :] = jnp.broadcast_to(seg_v[...].astype(F32), (keys.shape[1] - rope, tokens)).astype(BF16)
    for copy in loading[4:9]:
        copy.wait()
    lane = lax.broadcasted_iota(jnp.int32, (tokens, 128), 1)
    docs = lax.rem(lax.broadcasted_iota(jnp.int32, (128, tokens), 0), 64)
    own = (docs == jnp.broadcast_to(seg_v[...], (128, tokens))).astype(F32).T
    i = lax.broadcasted_iota(jnp.int32, (128, 128), 0)
    j = lax.broadcasted_iota(jnp.int32, (128, 128), 1)
    swap = jnp.where((j % 64 < 32) & (i == j + 32), -1.0, jnp.where((j % 64 >= 32) & (i == j - 32), 1.0, 0.0)).astype(BF16)
    cosine, sine = qc[...], qs[...]

    def turn(p, carry):
        raw = qr[:, pl.ds(pl.multiple_of(p * 128, 128), 128)]
        turned = raw.astype(F32) * cosine + nn(raw, swap) * sine
        qx[2 * p] = jnp.where(lane < 64, turned, own).astype(BF16)
        qx[2 * p + 1] = jnp.where(lane < 64, own, turned).astype(BF16)
        return carry

    lax.fori_loop(0, heads // 2, turn, 0)

    for slot, there in ((0, has0), (1, has1), (2, has2)):
        @pl.when(jnp.logical_not(there))
        def _(slot=slot):
            lat[slot] = jnp.zeros((tokens, width), BF16)
            keys[slot] = jnp.full(keys.shape[1:], -1.0, BF16)

    listeners = next2.astype(jnp.int32) + next3.astype(jnp.int32)
    pl.semaphore_wait(barrier, 7 + (n_z - 1) + listeners)

    ahead2 = remote(lat.at[3, mine], lat.at[1, mine], ahead_send.at[0], lat_recv.at[1, me], ctx + 2, me)
    ahead3 = remote(lat.at[3], lat.at[0], ahead_send.at[1], sib_recv.at[0], ctx + 3, me)
    keys2 = remote(keys.at[3], keys.at[1], keys_send.at[0], keys_recv.at[1], ctx + 2, me)
    keys3 = remote(keys.at[3], keys.at[0], keys_send.at[1], keys_recv.at[0], ctx + 3, me)
    keys_own = remote(keys.at[3], keys.at[2], keys_send.at[2], keys_recv.at[2], sibling, me)

    def hand(slot, h, to, i):
        return remote(lat.at[slot, rows_of(h)], lat.at[slot, rows_of(h)], lat_send.at[slot, i], lat_recv.at[slot, h], ctx, to)

    routes = [
        (me, beside), (me, along(me, 1)), (me, along(me, -1)),
        (beside, along(me, 1)), (beside, along(me, -1)),
        (along(me, -1), along(me, 1)), (along(beside, 1), along(me, -1)),
    ]

    def relay(slot, i):
        return hand(slot, *routes[i], i)

    def arrived(slot, h):
        hand(slot, h, beside, 0).wait_recv()

    def begin(slot):
        for i in range(3):
            relay(slot, i).start()

    def go_on(slot):
        arrived(slot, beside)
        relay(slot, 3).start()
        relay(slot, 4).start()
        arrived(slot, along(me, -1))
        relay(slot, 5).start()
        arrived(slot, along(beside, 1))
        relay(slot, 6).start()

    def complete(slot):
        for h in (along(me, 1), along(beside, -1), along(me, 2), along(beside, 2)):
            arrived(slot, h)

    @pl.when(next2)
    def _():
        ahead2.start()

    begin(3)

    @pl.when(next2)
    def _():
        keys2.start()

    @pl.when(next3)
    def _():
        keys3.start()

    @pl.when(core == 0)
    def _():
        keys_own.start()


    go_on(3)

    @pl.when(has1)
    def _():
        ahead2.wait_recv()
        begin(1)

    complete(3)
    pass_own = remote(lat.at[3], lat.at[2], sib_send.at[0], sib_recv.at[2], sibling, me)

    @pl.when(core == 0)
    def _():
        pass_own.start()

    @pl.when(next3)
    def _():
        ahead3.start()

    @pl.when(has1)
    def _():
        go_on(1)

    loading[3].wait()
    limit = prior_v[...].astype(BF16)
    for copy in loading[9:11]:
        copy.wait()

    def project(slot):
        at = pl.ds((slot - 1) * tokens, tokens)
        raw = lat[slot]
        clipped[...] = jnp.clip(raw, -limit, limit)
        def some(g, carry):
            c = clipped[...]
            up = nt(uk[pl.ds(4 * g, 4)].reshape(4 * hd, width), c) * gain
            kt[pl.ds(4 * g, 4), :, at] = up.astype(BF16).reshape(4, hd, tokens)
            for p in range(2):
                h = 4 * g + 2 * p
                both = nn(c, jnp.concatenate([uv[h], uv[h + 1]], axis=1)).astype(BF16)
                vals[h, at, :] = both[:, :hd]
                vals[h + 1, at, :] = both[:, hd:]
            return carry

        lax.fori_loop(0, heads // 4, some, 0)

    def turn_keys(slot):
        at = pl.ds(slot * tokens, tokens)
        a = keys[slot, 0:32, :].astype(F32)
        b = keys[slot, 32:64, :].astype(F32)
        cosine, sine = kc[:, at], ks[:, at]
        turned = jnp.concatenate([a * cosine - b * sine, b * cosine + a * sine], axis=0).astype(BF16)
        doc = jnp.broadcast_to(keys[slot, 64:80, :].astype(F32)[0:1, :], (64, tokens))
        number = lax.broadcasted_iota(jnp.int32, (64, tokens), 0).astype(F32)
        other = jnp.where(doc == number, 0.0, HIDDEN).astype(BF16)
        kx[0, 0:64, at] = turned
        kx[0, 64:128, at] = other
        kx[1, 0:64, at] = other
        kx[1, 64:128, at] = turned

    tops[kind] = jnp.max(jnp.abs(lat[3].astype(F32)), axis=0, keepdims=True)

    def spread_top(d):
        to = 4 * z + lax.rem(kind + d, 4)
        return remote(tops.at[kind], tops.at[kind], tops_send.at[d], tops_recv.at[kind], to, me)

    for d in (1, 2, 3):
        spread_top(d).start()
    project(3)
    turn_keys(3)

    to_core1 = remote(lat.at[1], lat.at[0], sib_send.at[1], sib_recv.at[0], sibling, me)
    to_core0 = remote(lat.at[1], lat.at[2], sib_send.at[1], sib_recv.at[2], sibling, me)
    keys_to_core1 = remote(keys.at[1], keys.at[0], keys_send.at[3], keys_recv.at[0], sibling, me)
    keys_to_core0 = remote(keys.at[1], keys.at[2], keys_send.at[3], keys_recv.at[2], sibling, me)

    @pl.when(has1)
    def _():
        complete(1)
        keys2.wait_recv()

        @pl.when(core == 0)
        def _():
            to_core1.start()
            keys_to_core1.start()

        @pl.when(core == 1)
        def _():
            to_core0.start()
            keys_to_core0.start()

    for d in (1, 2, 3):
        src = lax.rem(kind + d, 4)
        remote(tops.at[src], tops.at[src], tops_send.at[d], tops_recv.at[src], ctx, me).wait_recv()
    z_tops[z] = jnp.max(tops[...], axis=0)

    def spread_z(k):
        to = 4 * lax.rem(z + k, n_z) + kind
        return remote(z_tops.at[z], z_tops.at[z], z_send.at[k], z_recv.at[z], to, me)

    for k in range(1, n_z):
        spread_z(k).start()

    project(1)
    turn_keys(1)

    @pl.when(has2)
    def _():
        pass_own.wait_recv()
        keys_own.wait_recv()

    project(2)
    turn_keys(2)

    @pl.when(has0)
    def _():
        ahead3.wait_recv()
        keys3.wait_recv()

    oldest[...] = jnp.clip(lat[0], -limit, limit)
    turn_keys(0)

    doc = keys[3, 64:80, :].astype(F32)[0:1, 0:1]
    count = jnp.zeros((1, 1), F32)
    for slot in range(3):
        count += (keys[slot, 64:80, :].astype(F32)[0:1, tokens - 1:] == doc).astype(F32)
    seen[...] = jnp.broadcast_to(count, seen.shape)

    for k in range(1, n_z):
        src = lax.rem(z + k, n_z)
        remote(z_tops.at[src], z_tops.at[src], z_send.at[k], z_recv.at[src], ctx, me).wait_recv()
    amax_out[...] = jnp.max(z_tops[...], axis=0)
    qn_load.wait()

    for d in (1, 2, 3):
        spread_top(d).wait_send()
    for k in range(1, n_z):
        spread_z(k).wait_send()
    for i in range(7):
        relay(3, i).wait_send()

    @pl.when(next2)
    def _():
        ahead2.wait_send()
        keys2.wait_send()

    @pl.when(next3)
    def _():
        ahead3.wait_send()
        keys3.wait_send()

    @pl.when(has1)
    def _():
        for i in range(7):
            relay(1, i).wait_send()
        to_core1.wait_send()
        keys_to_core1.wait_send()

    @pl.when(core == 0)
    def _():
        keys_own.wait_send()
        pass_own.wait_send()


def attend(
    gain, seen, qn, qx, kt, kx, vals, oldest, uk, uv, amax, out, amax_out, kt0, vals0, outs, store, amax_store
):
    heads, hd, width = uk.shape
    tokens = qn.shape[0]
    write_amax = pltpu.make_async_copy(amax, amax_out, amax_store)
    write_amax.start()
    count = jnp.max(seen[...]).astype(jnp.int32)
    together = 4
    q_at = lax.broadcasted_iota(jnp.int32, (tokens, tokens), 0)
    k_at = lax.broadcasted_iota(jnp.int32, (tokens, tokens), 1)

    def write(p):
        some = pl.ds(pl.multiple_of(p * together * hd, together * hd), together * hd)
        return pltpu.make_async_copy(outs.at[:, some], out.at[:, some], store.at[p])

    @pl.when(count == 3)
    def _():
        def some(g, carry):
            c = oldest[...]
            up = nt(uk[pl.ds(4 * g, 4)].reshape(4 * hd, width), c) * gain
            kt0[pl.ds(4 * g, 4)] = up.astype(BF16).reshape(4, hd, tokens)
            for p in range(2):
                h = 4 * g + 2 * p
                both = nn(c, jnp.concatenate([uv[h], uv[h + 1]], axis=1)).astype(BF16)
                vals0[h] = both[:, :hd]
                vals0[h + 1] = both[:, hd:]
            return carry

        lax.fori_loop(0, heads // 4, some, 0)

    def with_blocks(blocks):
        past = blocks * tokens

        def group(g, carry):
            for i in range(together):
                h = together * g + i
                e = i % 2
                cols = pl.ds(pl.multiple_of(h * hd, hd), hd)
                q = jnp.concatenate([qn[:, cols], qx[h]], axis=1)
                if blocks == 3:
                    k = jnp.concatenate([kt0[h], kt[h]], axis=1)
                    v = jnp.concatenate([vals0[h], vals[h]], axis=0)
                else:
                    k = kt[h, :, (2 - blocks) * tokens:]
                    v = vals[h, (2 - blocks) * tokens:, :]
                k = jnp.concatenate([k, kx[e, :, (3 - blocks) * tokens:]], axis=0)
                s = nn(q, k)
                own = jnp.where(k_at <= q_at, s[:, past:], HIDDEN)
                s = jnp.concatenate([s[:, :past], own], axis=1) if blocks else own
                w = jnp.exp2(s - jnp.max(s, axis=1, keepdims=True)).astype(BF16)
                o = nn(w, jnp.concatenate([v, jnp.ones((past + tokens, hd), BF16)], axis=1))
                outs[:, cols] = (o[:, :hd] / o[:, hd:]).astype(BF16)
            write(g).start()
            return carry

        lax.fori_loop(0, heads // together, group, 0)

    for blocks in range(4):
        pl.when(count == blocks)(functools.partial(with_blocks, blocks))

    def written(p, carry):
        write(p).wait()
        return carry

    lax.fori_loop(0, heads // together, written, 0)
    write_amax.wait()


def shards(n_ctx, n_head, q_nope, q_rope, latent, amax_prior, k_rope, w_uk, w_uv, seg_ids):
    tokens, columns = q_nope.shape
    heads, hd, width = w_uk.shape
    rope = k_rope.shape[0]
    rows = latent.shape[0]
    gain = math.log2(math.e) * (hd + rope) ** -0.5
    q_cos, q_sin, k_cos, k_sin = tables(tokens, rope, gain)
    n_z = n_ctx // 4
    keys = BLOCKS * tokens
    dma = pltpu.SemaphoreType.DMA
    anywhere = pl.BlockSpec(memory_space=pl.ANY)
    in_vmem = pl.BlockSpec(memory_space=pltpu.VMEM)
    mib = 1024 * 1024
    operands = (
        latent, amax_prior.reshape(1, width), k_rope, seg_ids.reshape(1, tokens), q_nope, q_rope, w_uk, w_uv,
        jnp.asarray(q_cos), jnp.asarray(q_sin), jnp.asarray(k_cos), jnp.asarray(k_sin),
    )
    results = pl.pallas_call(
        functools.partial(kernel, n_ctx, n_head, gain),
        out_shape=(
            pltpu.VMEM((8, 128), F32),
            pltpu.VMEM((tokens, columns), BF16),
            pltpu.VMEM((heads, tokens, 128), BF16),
            pltpu.VMEM((heads, hd, keys - tokens), BF16),
            pltpu.VMEM((2, 128, keys), BF16),
            pltpu.VMEM((heads, keys - tokens, hd), BF16),
            pltpu.VMEM((tokens, width), BF16),
            pltpu.VMEM((heads, hd, width), BF16),
            pltpu.VMEM((heads, width, hd), BF16),
            pltpu.VMEM((1, width), F32),
        ),
        in_specs=[pl.BlockSpec(memory_space=pltpu.HBM)] * 12,
        out_specs=(in_vmem,) * 10,
        scratch_shapes=[
            pltpu.VMEM((BLOCKS, tokens, width), BF16),
            pltpu.VMEM((BLOCKS, rope + 16, tokens), BF16),
            pltpu.VMEM((4, 1, width), F32),
            pltpu.VMEM((n_z, 1, width), F32),
            pltpu.VMEM((1, width), F32),
            pltpu.VMEM((1, tokens), jnp.int32),
            pltpu.VMEM((tokens, heads * rope), BF16),
            pltpu.VMEM(q_cos.shape, F32),
            pltpu.VMEM(q_sin.shape, F32),
            pltpu.VMEM(k_cos.shape, F32),
            pltpu.VMEM(k_sin.shape, F32),
            pltpu.VMEM((tokens, width), BF16),
            dma((BLOCKS, n_head)),
            dma((BLOCKS, 7)),
            dma((2,)),
            dma((BLOCKS,)),
            dma((BLOCKS,)),
            dma((2,)),
            dma((BLOCKS,)),
            dma((4,)),
            dma((4,)),
            dma((n_z,)),
            dma((n_z,)),
            dma((12,)),
        ],
        compiler_params=pltpu.CompilerParams(collective_id=0, has_side_effects=True, vmem_limit_bytes=16 * mib),
        cost_estimate=pl.CostEstimate(flops=4_000_000_000, bytes_accessed=8_000_000, transcendentals=0),
    )(*(pltpu.with_memory_space_constraint(x, pltpu.HBM) for x in operands))
    attended, latent_amax = pl.pallas_call(
        functools.partial(attend, gain),
        out_shape=(jax.ShapeDtypeStruct((tokens, columns), BF16), jax.ShapeDtypeStruct((1, width), F32)),
        in_specs=[in_vmem] * 10,
        out_specs=(anywhere, anywhere),
        scratch_shapes=[
            pltpu.VMEM((heads, hd, tokens), BF16),
            pltpu.VMEM((heads, tokens, hd), BF16),
            pltpu.VMEM((tokens, columns), BF16),
            dma((heads // 2,)),
            dma,
        ],
        compiler_params=pltpu.CompilerParams(vmem_limit_bytes=24 * mib),
        cost_estimate=pl.CostEstimate(flops=10_000_000_000, bytes_accessed=8_000_000, transcendentals=4_194_304),
    )(*(pltpu.with_memory_space_constraint(x, pltpu.VMEM) for x in results))
    return attended, latent_amax.reshape(width)


def solution(mesh):
    placed = (
        P("ctx", "head"),
        P("ctx", "head"),
        P(("ctx", "head"), None),
        P(),
        P(None, "ctx"),
        P("head", None, None),
        P("head", None, None),
        P("ctx"),
    )
    return jax.shard_map(
        functools.partial(shards, mesh.shape["ctx"], mesh.shape["head"]),
        mesh=mesh, in_specs=placed, out_specs=(P("ctx", "head"), P()), check_vma=False,
    )
```

time: 208 us -> 37.5 us (0.18)
  blocking collectives: 119 us -> 0 us
  Pallas kernels: 0 us -> 36.7 us
  matrix products: 34.9 us -> 0 us
  starting transfers between devices: 28.4 us -> 0 us
  other arithmetic: 15.3 us -> 0 us
  local copies, waits for them, and re-layouts: 6.56 us -> 0 us
    pmax x1 -> x0, blocking collectives: 75.4 us -> none  [shards(): lax.pmax(jnp.max(jnp.abs(latent.astype(jnp.float32)), axis=0), ('ctx', 'h...]
    pallas_call x0 -> x2, Pallas kernels: none -> 36.7 us  [the longest x1 31.8 us: shards(): pl.pallas_call(functools.partial(kernel, n_ctx, n_head, gain), out_shape=...]
    dot_general x3 -> x0, matrix products: 34.9 us -> none  [the longest x1 14.5 us: shards(): jnp.einsum('thc,kc->thk', q_absorbed, lat_all, preferred_element_type=jnp...]
    ppermute x6 -> x0, starting transfers between devices: 28.4 us -> none  [from_behind(): return lax.ppermute(block, axis, route)]
    all_gather x1 -> x0, blocking collectives: 25.4 us -> none  [shards(): lax.all_gather(saturate(latent, amax_prior), 'head', axis=0, tiled=True)]
    unnamed x1 -> x0, blocking collectives: 18.7 us -> none
    reduce_sum x4 -> x0, other arithmetic: 10.3 us -> none  [the longest x1 7.69 us: shards(): denom = jnp.sum(exps, axis=-1)]
    unnamed x10 -> x0, local copies, waits for them, and re-layouts: 3.77 us -> none
  transfers between devices with their start and end apart: 6 -> 0, of which waited for: 0 -> 0; matrix products, arithmetic and copies ran while one was open for 7% -> 0% of each run, Pallas kernels for 0% -> 0%
where the time goes in v1:
time: 37.5 us; the launch traced here: 37.4 us
  Pallas kernels  36.7 us (98%)
  between operations  0.64 us (2%)
    pallas_call x1, Pallas kernels, shards(): pl.pallas_call(functools.partial(kernel, n_ctx, n_head, gain), out_shape=...  31.8 us
    pallas_call x1, Pallas kernels, shards(): pl.pallas_call(functools.partial(attend, gain), out_shape=(jax.ShapeDtype...  4.98 us

profile of v1, /device:TPU:1, one launch (start us, length us, event | category | flops | bytes accessed | tf_op | source)
XLA Modules:
  0.0 37.4 jit_solution(4278284940890709822)
XLA Ops:
  0.6 31.8 %shard_map.131 = (f32[8,128]{1,0:T(8,128)S(1)}, bf16[256,2048]{1,0:T(8,128)(2,1)S(1)}, bf16[16,256,128]{2,1,0:T(8,128)(2,1)S(1)}, bf16[16,128,768]{2,1,0:T(8,128...) custom-call(bf16[32,512]{1,0:T(8,128)(2,1)} %latent.1, ...), custom_call_target="tpu_custom_call" | custom-call | flops 4000000000 | bytes 8000000 | tf_op jit(solution)/shard_map/pallas_call | solution.py:447
  32.4 5.0 %shard_map.132 = (bf16[256,2048]{1,0:T(8,128)(2,1)}, f32[1,512]{1,0:T(1,128)}) custom-call(f32[8,128]{1,0:T(8,128)S(1)} %get-tuple-element.14.seen, bf16[256,2048]{1,0:T(8,128)(2,1)S(1)} %get-tuple-element.15.qn, bf16[16,256,128]{2,1,0:T(8,128)(2,1)S(1)} %get-tuple-element.16.qx, bf16[16,128,768]{2,1,0:T(8,128)(2,1)S(1)} %get-tuple-element.17.kt, ...), custom_call_target="tpu_custom_call" | custom-call | flops 10000000000 | bytes 8000000 | tf_op jit(solution)/shard_map/pallas_call | solution.py:492

commit v2 on v1

--- a/solution.py
+++ b/solution.py
@@ -41,9 +41,9 @@
     n_ctx, n_head, gain,
     latent, prior, k_rope, seg, q_nope, q_rope, w_uk, w_uv, q_cos, q_sin, k_cos, k_sin,
     seen, qn, qx, kt, kx, vals, oldest, uk, uv, amax_out,
-    lat, keys, tops, z_tops, prior_v, seg_v, qr, qc, qs, kc, ks, clipped,
-    lat_recv, lat_send, ahead_send, keys_recv, keys_send, sib_send, sib_recv,
-    tops_recv, tops_send, z_recv, z_send, load,
+    lat, keys, tops, z_tops, chain, prior_v, seg_v, qr, qc, qs, kc, ks, clipped,
+    pair_recv, pair_send, side_recv, side_send, far_recv, far_send, keys_recv, keys_send, sib_send, sib_recv,
+    tops_recv, tops_send, z_recv, z_send, chain_recv, chain_send, load,
 ):
     ctx = lax.axis_index("ctx")
     me = lax.axis_index("head")
@@ -69,9 +69,6 @@
     def along(h, d):
         return lax.rem(h + 2 * d + n_head, n_head)
 
-    def rows_of(h):
-        return pl.ds(pl.multiple_of(h * rows, rows), rows)
-
     def remote(src, dst, send, recv, c, h):
         return pltpu.make_async_remote_copy(
             src_ref=src, dst_ref=dst, send_sem=send, recv_sem=recv, device_id=(c, h), device_id_type=MESH
@@ -82,36 +79,69 @@
         (q_rope, qr), (q_cos, qc), (q_sin, qs), (k_cos, kc), (k_sin, ks), (w_uk, uk), (w_uv, uv), (q_nope, qn),
     ]
     loading = [pltpu.make_async_copy(src, dst, load.at[i]) for i, (src, dst) in enumerate(loads)]
-    for copy in loading:
+    for copy in loading[:9]:
         copy.start()
     qn_load = loading[11]
 
+    z_tops[...] = jnp.zeros_like(z_tops)
     barrier = pltpu.get_barrier_semaphore()
 
     def greet(c, h):
         pl.semaphore_signal(barrier, inc=1, device_id=(c, h), device_id_type=MESH)
 
-    for h in (beside, along(me, 1), along(me, -1)):
+    up, down = along(me, 1), along(me, -1)
+    for h in (beside, up, down):
         greet(ctx, h)
-    greet(sibling, me)
     for d in (1, 2, 3):
         greet(4 * z + lax.rem(kind + d, 4), me)
     for k in range(1, n_z):
-        greet(4 * lax.rem(z + k, n_z) + kind, me)
+        pl.when(z + k < n_z)(functools.partial(greet, ctx + 4 * k, me))
+    pl.when(z > 0)(functools.partial(greet, ctx - 4, me))
 
     @pl.when(has1)
     def _():
         greet(ctx - 2, me)
+        greet(ctx - 2, beside)
 
     @pl.when((core == 0) & has0)
     def _():
         greet(ctx - 3, me)
-
-    loading[0].wait()
-    loading[1].wait()
-    loading[2].wait()
-    keys[3, rope:, :] = jnp.broadcast_to(seg_v[...].astype(F32), (keys.shape[1] - rope, tokens)).astype(BF16)
-    for copy in loading[4:9]:
+        greet(ctx - 3, beside)
+
+    for slot, there in ((0, has0), (1, has1), (2, has2)):
+        @pl.when(jnp.logical_not(there))
+        def _(slot=slot):
+            lat[slot] = jnp.zeros((tokens, width), BF16)
+            keys[slot] = jnp.full(keys.shape[1:], -1.0, BF16)
+
+    listeners = 2 * (next2.astype(jnp.int32) + next3.astype(jnp.int32))
+    pl.semaphore_wait(barrier, 6 + listeners + z + (z < n_z - 1).astype(jnp.int32))
+
+    def chunk(slot, i, c, h):
+        return remote(latent, lat.at[slot, mine], pair_send.at[slot, i], pair_recv.at[slot, i], c, h)
+
+    chunk3 = chunk(3, 1, ctx, beside)
+    chunk1 = [chunk(1, 0, ctx + 2, me), chunk(1, 1, ctx + 2, beside)]
+    chunk0 = [chunk(0, 0, ctx + 3, me), chunk(0, 1, ctx + 3, beside)]
+    keys2 = remote(keys.at[3], keys.at[1], keys_send.at[0], keys_recv.at[1], ctx + 2, me)
+    keys3 = remote(keys.at[3], keys.at[0], keys_send.at[1], keys_recv.at[0], ctx + 3, me)
+    keys_own = remote(keys.at[3], keys.at[2], keys_send.at[2], keys_recv.at[2], sibling, me)
+    chunk3.start()
+
+    @pl.when(next2)
+    def _():
+        for copy in chunk1:
+            copy.start()
+
+    @pl.when(next3)
+    def _():
+        for copy in chunk0:
+            copy.start()
+
+    for copy in loading[9:]:
+        copy.start()
+
+    for copy in loading[:9]:
         copy.wait()
     lane = lax.broadcasted_iota(jnp.int32, (tokens, 128), 1)
     docs = lax.rem(lax.broadcasted_iota(jnp.int32, (128, tokens), 0), 64)
@@ -120,6 +150,7 @@
     j = lax.broadcasted_iota(jnp.int32, (128, 128), 1)
     swap = jnp.where((j % 64 < 32) & (i == j + 32), -1.0, jnp.where((j % 64 >= 32) & (i == j - 32), 1.0, 0.0)).astype(BF16)
     cosine, sine = qc[...], qs[...]
+    keys[3, rope:, :] = jnp.broadcast_to(seg_v[...].astype(F32), (keys.shape[1] - rope, tokens)).astype(BF16)
 
     def turn(p, carry):
         raw = qr[:, pl.ds(pl.multiple_of(p * 128, 128), 128)]
@@ -130,61 +161,98 @@
 
     lax.fori_loop(0, heads // 2, turn, 0)
 
-    for slot, there in ((0, has0), (1, has1), (2, has2)):
-        @pl.when(jnp.logical_not(there))
-        def _(slot=slot):
-            lat[slot] = jnp.zeros((tokens, width), BF16)
-            keys[slot] = jnp.full(keys.shape[1:], -1.0, BF16)
-
-    listeners = next2.astype(jnp.int32) + next3.astype(jnp.int32)
-    pl.semaphore_wait(barrier, 7 + (n_z - 1) + listeners)
-
-    ahead2 = remote(lat.at[3, mine], lat.at[1, mine], ahead_send.at[0], lat_recv.at[1, me], ctx + 2, me)
-    ahead3 = remote(lat.at[3], lat.at[0], ahead_send.at[1], sib_recv.at[0], ctx + 3, me)
-    keys2 = remote(keys.at[3], keys.at[1], keys_send.at[0], keys_recv.at[1], ctx + 2, me)
-    keys3 = remote(keys.at[3], keys.at[0], keys_send.at[1], keys_recv.at[0], ctx + 3, me)
-    keys_own = remote(keys.at[3], keys.at[2], keys_send.at[2], keys_recv.at[2], sibling, me)
-
-    def hand(slot, h, to, i):
-        return remote(lat.at[slot, rows_of(h)], lat.at[slot, rows_of(h)], lat_send.at[slot, i], lat_recv.at[slot, h], ctx, to)
-
-    routes = [
-        (me, beside), (me, along(me, 1)), (me, along(me, -1)),
-        (beside, along(me, 1)), (beside, along(me, -1)),
-        (along(me, -1), along(me, 1)), (along(beside, 1), along(me, -1)),
-    ]
-
-    def relay(slot, i):
-        return hand(slot, *routes[i], i)
-
-    def arrived(slot, h):
-        hand(slot, h, beside, 0).wait_recv()
-
-    def begin(slot):
-        for i in range(3):
-            relay(slot, i).start()
-
-    def go_on(slot):
-        arrived(slot, beside)
-        relay(slot, 3).start()
-        relay(slot, 4).start()
-        arrived(slot, along(me, -1))
-        relay(slot, 5).start()
-        arrived(slot, along(beside, 1))
-        relay(slot, 6).start()
-
-    def complete(slot):
-        for h in (along(me, 1), along(beside, -1), along(me, 2), along(beside, 2)):
-            arrived(slot, h)
+    def pair_at(h):
+        return pl.ds(pl.multiple_of(h // 2 * 2 * rows, 2 * rows), 2 * rows)
+
+    def one_at(h, x):
+        return pl.ds(pl.multiple_of((h // 2 * 2 + x) * rows, rows), rows)
+
+    def side(slots, i, to):
+        at = lat.at[slots, pair_at(me)]
+        return remote(at, at, side_send.at[slots.start, i], side_recv.at[slots.start, i], ctx, to)
+
+    def far(slots, i, h, to):
+        at = lat.at[slots, one_at(h, i)]
+        return remote(at, at, far_send.at[slots.start, i], far_recv.at[slots.start, i], ctx, to)
+
+    def sides(slots):
+        side(slots, 0, up).start()
+        side(slots, 1, down).start()
+
+    def passing(slots, piece):
+        if slots.start == 3:
+            routes = [(core == 0, 3, 2)]
+        else:
+            routes = [((core == 0) & has1, 1, 0), ((core == 1) & has1, 1, 2)]
+        at = [pair_at(me), pair_at(down), pair_at(up), one_at(along(me, 2), 0), one_at(along(me, 2), 1)][piece]
+        sems = sib_send.at[slots.start // 3, piece]
+        return [
+            (there, remote(lat.at[src, at], lat.at[dst, at], sems, sib_recv.at[dst, piece], sibling, me))
+            for there, src, dst in routes
+        ]
+
+    def pass_on(slots, piece):
+        for there, copy in passing(slots, piece):
+            pl.when(there)(copy.start)
+
+    def passed(slots):
+        for piece in range(5):
+            for there, copy in passing(slots, piece):
+                pl.when(there)(copy.wait_send)
+
+    def taken(dst):
+        for piece in range(5):
+            at = [pair_at(me), pair_at(down), pair_at(up), one_at(along(me, 2), 0), one_at(along(me, 2), 1)][piece]
+            remote(lat.at[dst, at], lat.at[dst, at], sib_send.at[0, piece], sib_recv.at[dst, piece], sibling, me).wait_recv()
+
+    def fars(slots):
+        side(slots, 0, up).wait_recv()
+        far(slots, 0, down, up).start()
+        side(slots, 1, down).wait_recv()
+        far(slots, 1, up, down).start()
+
+    def complete(slots):
+        far(slots, 0, down, up).wait_recv()
+        far(slots, 1, up, down).wait_recv()
+
+    def sent(slots):
+        for i in range(2):
+            side(slots, i, up).wait_send()
+            far(slots, i, up, up).wait_send()
+
+    own, late = pl.ds(3, 1), pl.ds(1, 1)
+    both = pl.ds(0, 2)
+    with_oldest = (core == 0) & has0
+    without_oldest = has1 & jnp.logical_not(with_oldest)
+
+    def earlier(act):
+        @pl.when(with_oldest)
+        def _():
+            act(both)
+
+        @pl.when(without_oldest)
+        def _():
+            act(late)
+
+    chunk3.wait_recv()
+    sides(own)
+    pass_on(own, 0)
+
+    @pl.when(has1)
+    def _():
+        for copy in chunk1:
+            copy.wait_recv()
+
+    @pl.when(with_oldest)
+    def _():
+        for copy in chunk0:
+            copy.wait_recv()
+
+    earlier(sides)
+    pass_on(late, 0)
 
     @pl.when(next2)
     def _():
-        ahead2.start()
-
-    begin(3)
-
-    @pl.when(next2)
-    def _():
         keys2.start()
 
     @pl.when(next3)
@@ -195,30 +263,16 @@
     def _():
         keys_own.start()
 
-
-    go_on(3)
-
-    @pl.when(has1)
-    def _():
-        ahead2.wait_recv()
-        begin(1)
-
-    complete(3)
-    pass_own = remote(lat.at[3], lat.at[2], sib_send.at[0], sib_recv.at[2], sibling, me)
-
-    @pl.when(core == 0)
-    def _():
-        pass_own.start()
-
-    @pl.when(next3)
-    def _():
-        ahead3.start()
-
-    @pl.when(has1)
-    def _():
-        go_on(1)
-
-    loading[3].wait()
+    fars(own)
+    pass_on(own, 1)
+    pass_on(own, 2)
+    earlier(fars)
+    pass_on(late, 1)
+    pass_on(late, 2)
+    complete(own)
+    pass_on(own, 3)
+    pass_on(own, 4)
+
     limit = prior_v[...].astype(BF16)
     for copy in loading[9:11]:
         copy.wait()
@@ -265,52 +319,67 @@
     project(3)
     turn_keys(3)
 
-    to_core1 = remote(lat.at[1], lat.at[0], sib_send.at[1], sib_recv.at[0], sibling, me)
-    to_core0 = remote(lat.at[1], lat.at[2], sib_send.at[1], sib_recv.at[2], sibling, me)
-    keys_to_core1 = remote(keys.at[1], keys.at[0], keys_send.at[3], keys_recv.at[0], sibling, me)
-    keys_to_core0 = remote(keys.at[1], keys.at[2], keys_send.at[3], keys_recv.at[2], sibling, me)
-
-    @pl.when(has1)
-    def _():
-        complete(1)
-        keys2.wait_recv()
-
-        @pl.when(core == 0)
-        def _():
-            to_core1.start()
-            keys_to_core1.start()
-
-        @pl.when(core == 1)
-        def _():
-            to_core0.start()
-            keys_to_core0.start()
-
     for d in (1, 2, 3):
         src = lax.rem(kind + d, 4)
         remote(tops.at[src], tops.at[src], tops_send.at[d], tops_recv.at[src], ctx, me).wait_recv()
     z_tops[z] = jnp.max(tops[...], axis=0)
 
     def spread_z(k):
-        to = 4 * lax.rem(z + k, n_z) + kind
-        return remote(z_tops.at[z], z_tops.at[z], z_send.at[k], z_recv.at[z], to, me)
+        return remote(z_tops.at[z], z_tops.at[z], z_send.at[k], z_recv.at[z], ctx - 4 * k, me)
 
     for k in range(1, n_z):
-        spread_z(k).start()
-
+        pl.when(z - k >= 0)(spread_z(k).start)
+
+    def step():
+        return remote(chain.at[1], chain.at[0], chain_send, chain_recv, ctx + 4, me)
+
+    def climb(point):
+        @pl.when(jnp.clip(z - n_z // 2, 0, 2) == point)
+        def _():
+            @pl.when(z == 0)
+            def _():
+                chain[1] = z_tops[z]
+
+            @pl.when(z > 0)
+            def _():
+                step().wait_recv()
+                chain[1] = jnp.maximum(chain[0], z_tops[z])
+
+            @pl.when(z < n_z - 1)
+            def _():
+                step().start()
+
+    climb(0)
+
+    keys_on = [
+        ((core == 0) & has1, remote(keys.at[1], keys.at[0], keys_send.at[3], keys_recv.at[0], sibling, me)),
+        ((core == 1) & has1, remote(keys.at[1], keys.at[2], keys_send.at[3], keys_recv.at[2], sibling, me)),
+    ]
+    earlier(complete)
+    pass_on(late, 3)
+    pass_on(late, 4)
+    pl.when(has1)(keys2.wait_recv)
+    for there, copy in keys_on:
+        pl.when(there)(copy.start)
     project(1)
     turn_keys(1)
+    climb(1)
 
     @pl.when(has2)
     def _():
-        pass_own.wait_recv()
+        taken(2)
         keys_own.wait_recv()
 
     project(2)
     turn_keys(2)
+    climb(2)
+
+    @pl.when((core == 1) & has0)
+    def _():
+        taken(0)
 
     @pl.when(has0)
     def _():
-        ahead3.wait_recv()
         keys3.wait_recv()
 
     oldest[...] = jnp.clip(lat[0], -limit, limit)
@@ -323,39 +392,40 @@
     seen[...] = jnp.broadcast_to(count, seen.shape)
 
     for k in range(1, n_z):
-        src = lax.rem(z + k, n_z)
-        remote(z_tops.at[src], z_tops.at[src], z_send.at[k], z_recv.at[src], ctx, me).wait_recv()
-    amax_out[...] = jnp.max(z_tops[...], axis=0)
+        @pl.when(z + k < n_z)
+        def _(k=k):
+            remote(z_tops.at[z + k], z_tops.at[z + k], z_send.at[k], z_recv.at[z + k], ctx, me).wait_recv()
+    amax_out[...] = jnp.maximum(jnp.max(z_tops[...], axis=0), chain[1])
     qn_load.wait()
 
     for d in (1, 2, 3):
         spread_top(d).wait_send()
     for k in range(1, n_z):
-        spread_z(k).wait_send()
-    for i in range(7):
-        relay(3, i).wait_send()
+        pl.when(z - k >= 0)(spread_z(k).wait_send)
+    pl.when(z < n_z - 1)(step().wait_send)
+    chunk3.wait_send()
+    sent(own)
+    earlier(sent)
 
     @pl.when(next2)
     def _():
-        ahead2.wait_send()
+        for copy in chunk1:
+            copy.wait_send()
         keys2.wait_send()
 
     @pl.when(next3)
     def _():
-        ahead3.wait_send()
+        for copy in chunk0:
+            copy.wait_send()
         keys3.wait_send()
 
-    @pl.when(has1)
-    def _():
-        for i in range(7):
-            relay(1, i).wait_send()
-        to_core1.wait_send()
-        keys_to_core1.wait_send()
+    passed(own)
+    passed(late)
+    pl.when(has1)(keys_on[0][1].wait_send)
 
     @pl.when(core == 0)
     def _():
         keys_own.wait_send()
-        pass_own.wait_send()
 
 
 def attend(
@@ -366,12 +436,12 @@
     write_amax = pltpu.make_async_copy(amax, amax_out, amax_store)
     write_amax.start()
     count = jnp.max(seen[...]).astype(jnp.int32)
-    together = 4
+    together = min(heads, 8)
     q_at = lax.broadcasted_iota(jnp.int32, (tokens, tokens), 0)
     k_at = lax.broadcasted_iota(jnp.int32, (tokens, tokens), 1)
 
     def write(p):
-        some = pl.ds(pl.multiple_of(p * together * hd, together * hd), together * hd)
+        some = pl.ds(pl.multiple_of(p * 4 * hd, 4 * hd), 4 * hd)
         return pltpu.make_async_copy(outs.at[:, some], out.at[:, some], store.at[p])
 
     @pl.when(count == 3)
@@ -411,7 +481,8 @@
                 w = jnp.exp2(s - jnp.max(s, axis=1, keepdims=True)).astype(BF16)
                 o = nn(w, jnp.concatenate([v, jnp.ones((past + tokens, hd), BF16)], axis=1))
                 outs[:, cols] = (o[:, :hd] / o[:, hd:]).astype(BF16)
-            write(g).start()
+                if i % 4 == 3:
+                    write(together // 4 * g + i // 4).start()
             return carry
 
         lax.fori_loop(0, heads // together, group, 0)
@@ -423,7 +494,7 @@
         write(p).wait()
         return carry
 
-    lax.fori_loop(0, heads // together, written, 0)
+    lax.fori_loop(0, heads // 4, written, 0)
     write_amax.wait()
 
 
@@ -465,6 +536,7 @@
             pltpu.VMEM((BLOCKS, rope + 16, tokens), BF16),
             pltpu.VMEM((4, 1, width), F32),
             pltpu.VMEM((n_z, 1, width), F32),
+            pltpu.VMEM((2, 1, width), F32),
             pltpu.VMEM((1, width), F32),
             pltpu.VMEM((1, tokens), jnp.int32),
             pltpu.VMEM((tokens, heads * rope), BF16),
@@ -473,17 +545,22 @@
             pltpu.VMEM(k_cos.shape, F32),
             pltpu.VMEM(k_sin.shape, F32),
             pltpu.VMEM((tokens, width), BF16),
-            dma((BLOCKS, n_head)),
-            dma((BLOCKS, 7)),
-            dma((2,)),
+            dma((BLOCKS, 2)),
+            dma((BLOCKS, 2)),
+            dma((BLOCKS, 2)),
+            dma((BLOCKS, 2)),
+            dma((BLOCKS, 2)),
+            dma((BLOCKS, 2)),
             dma((BLOCKS,)),
             dma((BLOCKS,)),
-            dma((2,)),
-            dma((BLOCKS,)),
+            dma((2, 5)),
+            dma((BLOCKS, 5)),
             dma((4,)),
             dma((4,)),
             dma((n_z,)),
             dma((n_z,)),
+            dma,
+            dma,
             dma((12,)),
         ],
         compiler_params=pltpu.CompilerParams(collective_id=0, has_side_effects=True, vmem_limit_bytes=16 * mib),
@@ -498,7 +575,7 @@
             pltpu.VMEM((heads, hd, tokens), BF16),
             pltpu.VMEM((heads, tokens, hd), BF16),
             pltpu.VMEM((tokens, columns), BF16),
-            dma((heads // 2,)),
+            dma((heads // 4,)),
             dma,
         ],
         compiler_params=pltpu.CompilerParams(vmem_limit_bytes=24 * mib),

time: 37.5 us -> 39.9 us (1.064)
  the two profiles are of different devices: /device:TPU:1 before, /device:TPU:224 now
where the time goes in v2:
time: 39.9 us; the launch traced here: 39.8 us
  Pallas kernels  39.2 us (98%)
  between operations  0.64 us (2%)
    pallas_call x1, Pallas kernels, shards(): pl.pallas_call(functools.partial(kernel, n_ctx, n_head, gain), out_shape=...  35 us
    pallas_call x1, Pallas kernels, shards(): pl.pallas_call(functools.partial(attend, gain), out_shape=(jax.ShapeDtype...  4.17 us

profile of v2, /device:TPU:224, one launch (start us, length us, event | category | flops | bytes accessed | tf_op | source)
XLA Modules:
  0.0 39.8 jit_solution(10870562960487696344)
XLA Ops:
  0.6 35.0 %shard_map.131 = (f32[8,128]{1,0:T(8,128)S(1)}, bf16[256,2048]{1,0:T(8,128)(2,1)S(1)}, bf16[16,256,128]{2,1,0:T(8,128)(2,1)S(1)}, bf16[16,128,768]{2,1,0:T(8,128...) custom-call(bf16[32,512]{1,0:T(8,128)(2,1)} %latent.1, ...), custom_call_target="tpu_custom_call" | custom-call | flops 4000000000 | bytes 8000000 | tf_op jit(solution)/shard_map/pallas_call | solution.py:518
  35.7 4.2 %shard_map.132 = (bf16[256,2048]{1,0:T(8,128)(2,1)}, f32[1,512]{1,0:T(1,128)}) custom-call(f32[8,128]{1,0:T(8,128)S(1)} %get-tuple-element.14.seen, bf16[256,2048]{1,0:T(8,128)(2,1)S(1)} %get-tuple-element.15.qn, bf16[16,256,128]{2,1,0:T(8,128)(2,1)S(1)} %get-tuple-element.16.qx, bf16[16,128,768]{2,1,0:T(8,128)(2,1)S(1)} %get-tuple-element.17.kt, ...), custom_call_target="tpu_custom_call" | custom-call | flops 10000000000 | bytes 8000000 | tf_op jit(solution)/shard_map/pallas_call | solution.py:569

commit v3 on v2

v3 whole, which is shorter than its diff:
```python
import functools
import math

import jax
import jax.numpy as jnp
import numpy as np
from jax import lax
from jax.experimental import pallas as pl
from jax.experimental.pallas import tpu as pltpu
from jax.sharding import PartitionSpec as P

MESH = pl.DeviceIdType.MESH
BF16 = jnp.bfloat16
F32 = jnp.float32
BLOCKS = 4
HIDDEN = -1e30


def tables(tokens, rope, gain):
    half = rope // 2
    freq = np.exp(np.arange(half) * (-2.0 * math.log(10000.0) / rope))
    q_angle = np.arange(tokens)[:, None] * freq[None, :]
    q_cos = np.tile(np.cos(q_angle), (1, 4)).astype(np.float32)
    q_sin = np.tile(np.sin(q_angle), (1, 4)).astype(np.float32)
    k_place = np.arange(BLOCKS * tokens) - (BLOCKS - 1) * tokens
    k_angle = freq[:, None] * k_place[None, :]
    k_cos = (np.cos(k_angle) * gain).astype(np.float32)
    k_sin = (np.sin(k_angle) * gain).astype(np.float32)
    return q_cos, q_sin, k_cos, k_sin


def nt(a, b):
    return lax.dot_general(a, b, (((1,), (1,)), ((), ())), preferred_element_type=F32)


def nn(a, b):
    return jnp.dot(a, b, preferred_element_type=F32)


def kernel(
    n_ctx, n_head, gain,
    latent, prior, k_rope, seg, q_nope, q_rope, w_uk, w_uv, q_cos, q_sin, k_cos, k_sin,
    seen, own_out, own_top, qn, qx, kt, kx, vals, oldest, uk, uv, amax_out,
    lat, tops, z_tops, prior_v, seg_v, qr, qc, qs, kc, ks, clipped, kt3, vals3,
    own_recv, own_send, pair_recv, pair_send, side_recv, side_send, far_recv, far_send,
    sib_send, sib_recv, tops_recv, tops_send, z_recv, z_send, load,
):
    ctx = lax.axis_index("ctx")
    me = lax.axis_index("head")
    core = lax.rem(ctx, 2)
    sibling = ctx + 1 - 2 * core
    n_z = n_ctx // 4
    z = ctx // 4
    heads, hd, width = uk.shape
    tokens = qn.shape[0]
    rope = k_rope.shape[0]
    rows = latent.shape[0]
    half = rope // 2
    mine = pl.ds(pl.multiple_of(me * rows, rows), rows)
    block = pl.ds(0, tokens)
    key_rows = pl.ds(tokens, half + 16)

    kind = lax.rem(ctx, 4)
    has1 = ctx >= 2
    has2 = (core == 1) | (ctx >= 2)
    has0 = ctx >= 3
    next2 = ctx + 2 < n_ctx
    next3 = (core == 1) & (ctx + 3 < n_ctx)

    beside = me + 1 - 2 * lax.rem(me, 2)
    up = lax.rem(me + 2, n_head)
    down = lax.rem(me + n_head - 2, n_head)

    def remote(src, dst, send, recv, c, h):
        return pltpu.make_async_remote_copy(
            src_ref=src, dst_ref=dst, send_sem=send, recv_sem=recv, device_id=(c, h), device_id_type=MESH
        )

    loads = [
        (latent, lat.at[3, mine]),
        (k_rope.at[pl.ds(0, half)], lat.at[3, pl.ds(tokens, half), pl.ds(0, tokens)]),
        (k_rope.at[pl.ds(half, half)], lat.at[3, pl.ds(tokens, half), pl.ds(tokens, tokens)]),
        (seg, seg_v), (prior, prior_v),
        (q_rope, qr), (q_cos, qc), (q_sin, qs), (k_cos, kc), (k_sin, ks), (w_uk, uk), (w_uv, uv), (q_nope, qn),
    ]
    loading = [pltpu.make_async_copy(src, dst, load.at[i]) for i, (src, dst) in enumerate(loads)]
    for copy in loading[:10]:
        copy.start()

    barrier = pltpu.get_barrier_semaphore()

    def greet(c, h):
        pl.semaphore_signal(barrier, inc=1, device_id=(c, h), device_id_type=MESH)

    @pl.when(has1)
    def _():
        greet(ctx - 2, me)
        greet(ctx - 2, beside)

    @pl.when((core == 0) & has0)
    def _():
        greet(ctx - 3, me)
        greet(ctx - 3, beside)

    for k in range(1, n_head):
        greet(ctx, lax.rem(me + k, n_head))
    for d in (1, 2, 3):
        greet(4 * z + lax.rem(kind + d, 4), me)
    for k in range(1, n_z):
        greet(4 * lax.rem(z + k, n_z) + kind, me)

    for slot, there in ((0, has0), (1, has1), (2, has2)):
        @pl.when(jnp.logical_not(there))
        def _(slot=slot):
            lat[slot, block, :] = jnp.zeros((tokens, width), BF16)
            lat[slot, key_rows, :] = jnp.full((half + 16, width), -1.0, BF16)

    for copy in loading[:4]:
        copy.wait()
    lat[3, pl.ds(tokens + half, 16), :] = jnp.broadcast_to(
        jnp.concatenate([seg_v[...], seg_v[...]], axis=1).astype(F32), (16, width)
    ).astype(BF16)
    listeners = 2 * (next2.astype(jnp.int32) + next3.astype(jnp.int32))
    pl.semaphore_wait(barrier, n_head - 1 + 3 + (n_z - 1) + listeners)

    def share(k):
        return remote(
            lat.at[3, mine], lat.at[3, mine], own_send, own_recv, ctx, lax.rem(me + k, n_head)
        )

    def chunk(slot, i, c, h):
        return remote(lat.at[3, mine], lat.at[slot, mine], pair_send.at[slot, i], pair_recv.at[slot, i], c, h)

    def keys_to(slot, c):
        return remote(lat.at[3, key_rows], lat.at[slot, key_rows], pair_send.at[slot, 2], pair_recv.at[slot, 2], c, me)

    ahead2 = [chunk(1, 0, ctx + 2, me), chunk(1, 1, ctx + 2, beside), keys_to(1, ctx + 2)]
    ahead3 = [chunk(0, 0, ctx + 3, me), chunk(0, 1, ctx + 3, beside), keys_to(0, ctx + 3)]

    @pl.when(next2)
    def _():
        for copy in ahead2:
            copy.start()

    for k in range(1, n_head):
        share(k).start()

    @pl.when(next3)
    def _():
        for copy in ahead3:
            copy.start()

    for copy in loading[10:]:
        copy.start()

    for copy in loading[4:10]:
        copy.wait()
    lane = lax.broadcasted_iota(jnp.int32, (tokens, 128), 1)
    docs = lax.broadcasted_iota(jnp.int32, (64, tokens), 0)
    docs = jnp.concatenate([docs, docs], axis=0)
    mark = (docs == jnp.broadcast_to(seg_v[...], (128, tokens))).astype(F32).T
    i = lax.broadcasted_iota(jnp.int32, (128, 128), 0)
    j = lax.broadcasted_iota(jnp.int32, (128, 128), 1)
    low = (j & 63) < 32
    swap = jnp.where(low & (i == j + 32), -1.0, jnp.where(jnp.logical_not(low) & (i == j - 32), 1.0, 0.0)).astype(BF16)
    cosine, sine = qc[...], qs[...]

    def turn(p, carry):
        raw = qr[:, pl.ds(pl.multiple_of(p * 128, 128), 128)]
        turned = raw.astype(F32) * cosine + nn(raw, swap) * sine
        qx[2 * p] = jnp.where(lane < 64, turned, mark).astype(BF16)
        qx[2 * p + 1] = jnp.where(lane < 64, mark, turned).astype(BF16)
        return carry

    lax.fori_loop(0, heads // 2, turn, 0, unroll=2)

    def pair_at(h):
        return pl.ds(pl.multiple_of(h // 2 * 2 * rows, 2 * rows), 2 * rows)

    def one_at(h, x):
        return pl.ds(pl.multiple_of((h // 2 * 2 + x) * rows, rows), rows)

    def side(slots, i, to):
        at = lat.at[slots, pair_at(me)]
        return remote(at, at, side_send.at[i], side_recv.at[i], ctx, to)

    def far(slots, i, h, to):
        at = lat.at[slots, one_at(h, i)]
        return remote(at, at, far_send.at[i], far_recv.at[i], ctx, to)

    def sides(slots):
        side(slots, 0, up).start()
        side(slots, 1, down).start()

    def fars(slots):
        side(slots, 0, up).wait_recv()
        far(slots, 0, down, up).start()
        side(slots, 1, down).wait_recv()
        far(slots, 1, up, down).start()

    def complete(slots):
        far(slots, 0, down, up).wait_recv()
        far(slots, 1, up, down).wait_recv()

    def sent(slots):
        for i in range(2):
            side(slots, i, up).wait_send()
            far(slots, i, up, up).wait_send()

    with_oldest = (core == 0) & has0
    without_oldest = has1 & jnp.logical_not(with_oldest)

    def earlier(act):
        pl.when(with_oldest)(functools.partial(act, pl.ds(0, 2)))
        pl.when(without_oldest)(functools.partial(act, pl.ds(1, 1)))

    @pl.when(has1)
    def _():
        for copy in ahead2:
            copy.wait_recv()

    @pl.when(with_oldest)
    def _():
        for copy in ahead3:
            copy.wait_recv()

    earlier(sides)

    others = lat.at[3, pl.ds(0, (n_head - 1) * rows)]
    remote(others, others, own_send, own_recv, ctx, me).wait_recv()
    pass_own = remote(lat.at[3], lat.at[2], sib_send.at[0], sib_recv.at[2], sibling, me)
    pl.when(core == 0)(pass_own.start)
    tops[kind] = jnp.max(jnp.abs(lat[3, block, :].astype(F32)), axis=0, keepdims=True)

    def spread_top(d):
        return remote(tops.at[kind], tops.at[kind], tops_send, tops_recv, 4 * z + lax.rem(kind + d, 4), me)

    for d in (1, 2, 3):
        spread_top(d).start()

    limit = prior_v[...].astype(BF16)
    for copy in loading[10:]:
        copy.wait()

    def project(slot):
        at = pl.ds((slot - 1) * tokens, tokens)
        clipped[...] = jnp.clip(lat[slot, block, :], -limit, limit)

        def some(g, carry):
            c = clipped[...]
            ups = (nt(uk[pl.ds(4 * g, 4)].reshape(4 * hd, width), c) * gain).astype(BF16).reshape(4, hd, tokens)
            if slot == 3:
                kt3[pl.ds(4 * g, 4)] = ups
            else:
                kt[pl.ds(4 * g, 4), :, at] = ups
            for p in range(2):
                h = 4 * g + 2 * p
                both = nn(c, jnp.concatenate([uv[h], uv[h + 1]], axis=1)).astype(BF16)
                for e in range(2):
                    if slot == 3:
                        vals3[h + e] = both[:, e * hd:(e + 1) * hd]
                    else:
                        vals[h + e, at, :] = both[:, e * hd:(e + 1) * hd]
            return carry

        lax.fori_loop(0, heads // 4, some, 0)

    def turn_keys(slot):
        at = pl.ds(slot * tokens, tokens)
        a = lat[slot, pl.ds(tokens, half), 0:tokens].astype(F32)
        b = lat[slot, pl.ds(tokens, half), tokens:2 * tokens].astype(F32)
        cosine, sine = kc[:, at], ks[:, at]
        turned = jnp.concatenate([a * cosine - b * sine, b * cosine + a * sine], axis=0).astype(BF16)
        doc = jnp.broadcast_to(lat[slot, pl.ds(tokens + half, 16), 0:tokens].astype(F32)[0:1, :], (64, tokens))
        number = lax.broadcasted_iota(jnp.int32, (64, tokens), 0).astype(F32)
        other = jnp.where(doc == number, 0.0, HIDDEN).astype(BF16)
        kx[0, 0:64, at] = turned
        kx[0, 64:128, at] = other
        kx[1, 0:64, at] = other
        kx[1, 64:128, at] = turned

    project(3)
    turn_keys(3)
    earlier(fars)

    q_at = lax.broadcasted_iota(jnp.int32, (tokens, tokens), 0)
    k_at = lax.broadcasted_iota(jnp.int32, (tokens, tokens), 1)

    def attend_own(first):
        for h in range(first, first + heads // 2):
            q = jnp.concatenate([qn[:, h * hd:(h + 1) * hd], qx[h]], axis=1)
            k = jnp.concatenate([kt3[h], kx[h % 2, :, 3 * tokens:]], axis=0)
            s = jnp.where(k_at <= q_at, nn(q, k), HIDDEN)
            top = jnp.max(s, axis=1, keepdims=True)
            w = jnp.exp2(s - top).astype(BF16)
            own_out[h] = nn(w, jnp.concatenate([vals3[h], jnp.ones((tokens, hd), BF16)], axis=1))
            own_top[h] = jnp.broadcast_to(top, (tokens, hd))

    attend_own(0)

    three = tops.at[pl.ds(0, 3)]
    remote(three, three, tops_send, tops_recv, ctx, me).wait_recv()
    z_tops[z] = jnp.max(tops[...], axis=0)

    def spread_z(k):
        return remote(z_tops.at[z], z_tops.at[z], z_send, z_recv, 4 * lax.rem(z + k, n_z) + kind, me)

    for k in range(1, n_z):
        spread_z(k).start()

    earlier(complete)
    on = [
        ((core == 0) & has1, remote(lat.at[1], lat.at[0], sib_send.at[1], sib_recv.at[0], sibling, me)),
        ((core == 1) & has1, remote(lat.at[1], lat.at[2], sib_send.at[1], sib_recv.at[2], sibling, me)),
    ]
    for there, copy in on:
        pl.when(there)(copy.start)

    attend_own(heads // 2)
    project(1)
    turn_keys(1)

    pl.when(has2)(pass_own.wait_recv)
    project(2)
    turn_keys(2)

    pl.when((core == 1) & has0)(on[0][1].wait_recv)
    oldest[...] = jnp.clip(lat[0, block, :], -limit, limit)
    turn_keys(0)

    doc_at = pl.ds(tokens + half, 16)
    doc = lat[3, doc_at, 0:tokens].astype(F32)[0:1, 0:1]
    count = jnp.zeros((1, 1), F32)
    for slot in range(3):
        count += (lat[slot, doc_at, 0:tokens].astype(F32)[0:1, tokens - 1:] == doc).astype(F32)
    seen[...] = jnp.broadcast_to(count, seen.shape)

    rest = z_tops.at[pl.ds(0, n_z - 1)]
    remote(rest, rest, z_send, z_recv, ctx, me).wait_recv()
    amax_out[...] = jnp.max(z_tops[...], axis=0)

    remote(others, others, own_send, own_recv, ctx, me).wait_send()
    remote(three, three, tops_send, tops_recv, ctx, me).wait_send()
    remote(rest, rest, z_send, z_recv, ctx, me).wait_send()
    earlier(sent)

    @pl.when(next2)
    def _():
        for copy in ahead2:
            copy.wait_send()

    @pl.when(next3)
    def _():
        for copy in ahead3:
            copy.wait_send()

    pl.when(core == 0)(pass_own.wait_send)
    pl.when(has1)(on[0][1].wait_send)


def attend(
    gain, seen, own_out, own_top, qn, qx, kt, kx, vals, oldest, uk, uv, amax,
    out, amax_out, kt0, vals0, outs, store, amax_store,
):
    heads, hd, width = uk.shape
    tokens = qn.shape[0]
    write_amax = pltpu.make_async_copy(amax, amax_out, amax_store)
    write_amax.start()
    count = jnp.max(seen[...]).astype(jnp.int32)
    together = min(heads, 8)

    def write(p):
        some = pl.ds(pl.multiple_of(p * 4 * hd, 4 * hd), 4 * hd)
        return pltpu.make_async_copy(outs.at[:, some], out.at[:, some], store.at[p])

    @pl.when(count == 3)
    def _():
        def some(g, carry):
            c = oldest[...]
            ups = nt(uk[pl.ds(4 * g, 4)].reshape(4 * hd, width), c) * gain
            kt0[pl.ds(4 * g, 4)] = ups.astype(BF16).reshape(4, hd, tokens)
            for p in range(2):
                h = 4 * g + 2 * p
                both = nn(c, jnp.concatenate([uv[h], uv[h + 1]], axis=1)).astype(BF16)
                vals0[h] = both[:, :hd]
                vals0[h + 1] = both[:, hd:]
            return carry

        lax.fori_loop(0, heads // 4, some, 0)

    def with_blocks(blocks):
        def group(g, carry):
            for i in range(together):
                h = together * g + i
                e = i % 2
                cols = pl.ds(pl.multiple_of(h * hd, hd), hd)
                o = own_out[h]
                if blocks:
                    q = jnp.concatenate([qn[:, cols], qx[h]], axis=1)
                    if blocks == 3:
                        k = jnp.concatenate([kt0[h], kt[h]], axis=1)
                        v = jnp.concatenate([vals0[h], vals[h]], axis=0)
                    else:
                        k = kt[h, :, (2 - blocks) * tokens:]
                        v = vals[h, (2 - blocks) * tokens:, :]
                    k = jnp.concatenate([k, kx[e, :, (3 - blocks) * tokens:3 * tokens]], axis=0)
                    s = nn(q, k)
                    own = own_top[h]
                    top = jnp.maximum(jnp.max(s, axis=1, keepdims=True), own[:, 0:1])
                    w = jnp.exp2(s - top).astype(BF16)
                    scale = jnp.exp2(own - top)
                    o = o * jnp.concatenate([scale, scale], axis=1) + nn(
                        w, jnp.concatenate([v, jnp.ones((blocks * tokens, hd), BF16)], axis=1)
                    )
                outs[:, cols] = (o[:, :hd] / o[:, hd:]).astype(BF16)
                if i % 4 == 3:
                    write(together // 4 * g + i // 4).start()
            return carry

        lax.fori_loop(0, heads // together, group, 0)

    for blocks in range(4):
        pl.when(count == blocks)(functools.partial(with_blocks, blocks))

    def written(p, carry):
        write(p).wait()
        return carry

    lax.fori_loop(0, heads // 4, written, 0)
    write_amax.wait()


def shards(n_ctx, n_head, q_nope, q_rope, latent, amax_prior, k_rope, w_uk, w_uv, seg_ids):
    tokens, columns = q_nope.shape
    heads, hd, width = w_uk.shape
    rope = k_rope.shape[0]
    rows = latent.shape[0]
    gain = math.log2(math.e) * (hd + rope) ** -0.5
    q_cos, q_sin, k_cos, k_sin = tables(tokens, rope, gain)
    n_z = n_ctx // 4
    keys = BLOCKS * tokens
    dma = pltpu.SemaphoreType.DMA
    anywhere = pl.BlockSpec(memory_space=pl.ANY)
    in_vmem = pl.BlockSpec(memory_space=pltpu.VMEM)
    mib = 1024 * 1024
    operands = (
        latent, amax_prior.reshape(1, width), k_rope, seg_ids.reshape(1, tokens), q_nope, q_rope, w_uk, w_uv,
        jnp.asarray(q_cos), jnp.asarray(q_sin), jnp.asarray(k_cos), jnp.asarray(k_sin),
    )
    results = pl.pallas_call(
        functools.partial(kernel, n_ctx, n_head, gain),
        out_shape=(
            pltpu.VMEM((8, 128), F32),
            pltpu.VMEM((heads, tokens, 2 * hd), F32),
            pltpu.VMEM((heads, tokens, hd), F32),
            pltpu.VMEM((tokens, columns), BF16),
            pltpu.VMEM((heads, tokens, 128), BF16),
            pltpu.VMEM((heads, hd, 2 * tokens), BF16),
            pltpu.VMEM((2, 128, keys), BF16),
            pltpu.VMEM((heads, 2 * tokens, hd), BF16),
            pltpu.VMEM((tokens, width), BF16),
            pltpu.VMEM((heads, hd, width), BF16),
            pltpu.VMEM((heads, width, hd), BF16),
            pltpu.VMEM((1, width), F32),
        ),
        in_specs=[pl.BlockSpec(memory_space=pltpu.HBM)] * 12,
        out_specs=(in_vmem,) * 12,
        scratch_shapes=[
            pltpu.VMEM((BLOCKS, tokens + rope // 2 + 16, width), BF16),
            pltpu.VMEM((4, 1, width), F32),
            pltpu.VMEM((n_z, 1, width), F32),
            pltpu.VMEM((1, width), F32),
            pltpu.VMEM((1, tokens), jnp.int32),
            pltpu.VMEM((tokens, heads * rope), BF16),
            pltpu.VMEM(q_cos.shape, F32),
            pltpu.VMEM(q_sin.shape, F32),
            pltpu.VMEM(k_cos.shape, F32),
            pltpu.VMEM(k_sin.shape, F32),
            pltpu.VMEM((tokens, width), BF16),
            pltpu.VMEM((heads, hd, tokens), BF16),
            pltpu.VMEM((heads, tokens, hd), BF16),
            dma,
            dma,
            dma((2, 3)),
            dma((2, 3)),
            dma((2,)),
            dma((2,)),
            dma((2,)),
            dma((2,)),
            dma((2,)),
            dma((BLOCKS,)),
            dma,
            dma,
            dma,
            dma,
            dma((13,)),
        ],
        compiler_params=pltpu.CompilerParams(collective_id=0, has_side_effects=True, vmem_limit_bytes=18 * mib),
        cost_estimate=pl.CostEstimate(flops=4_000_000_000, bytes_accessed=8_000_000, transcendentals=0),
    )(*(pltpu.with_memory_space_constraint(x, pltpu.HBM) for x in operands))
    attended, latent_amax = pl.pallas_call(
        functools.partial(attend, gain),
        out_shape=(jax.ShapeDtypeStruct((tokens, columns), BF16), jax.ShapeDtypeStruct((1, width), F32)),
        in_specs=[in_vmem] * 12,
        out_specs=(anywhere, anywhere),
        scratch_shapes=[
            pltpu.VMEM((heads, hd, tokens), BF16),
            pltpu.VMEM((heads, tokens, hd), BF16),
            pltpu.VMEM((tokens, columns), BF16),
            dma((heads // 4,)),
            dma,
        ],
        compiler_params=pltpu.CompilerParams(vmem_limit_bytes=18 * mib),
        cost_estimate=pl.CostEstimate(flops=10_000_000_000, bytes_accessed=8_000_000, transcendentals=4_194_304),
    )(*(pltpu.with_memory_space_constraint(x, pltpu.VMEM) for x in results))
    return attended, latent_amax.reshape(width)


def solution(mesh):
    placed = (
        P("ctx", "head"),
        P("ctx", "head"),
        P(("ctx", "head"), None),
        P(),
        P(None, "ctx"),
        P("head", None, None),
        P("head", None, None),
        P("ctx"),
    )
    return jax.shard_map(
        functools.partial(shards, mesh.shape["ctx"], mesh.shape["head"]),
        mesh=mesh, in_specs=placed, out_specs=(P("ctx", "head"), P()), check_vma=False,
    )
```

time: 39.9 us -> 34.9 us (0.87)
  the two profiles are of different devices: /device:TPU:224 before, /device:TPU:32 now
where the time goes in v3:
time: 34.9 us; the launch traced here: 34.8 us
  Pallas kernels  34.2 us (98%)
  between operations  0.64 us (2%)
    pallas_call x1, Pallas kernels, shards(): pl.pallas_call(functools.partial(kernel, n_ctx, n_head, gain), out_shape=...  28.6 us
    pallas_call x1, Pallas kernels, shards(): pl.pallas_call(functools.partial(attend, gain), out_shape=(jax.ShapeDtype...  5.55 us

profile of v3, /device:TPU:32, one launch (start us, length us, event | category | flops | bytes accessed | tf_op | source)
XLA Modules:
  0.0 34.8 jit_solution(13148675790220650975)
XLA Ops:
  0.6 28.6 %shard_map.131 = (f32[8,128]{1,0:T(8,128)S(1)}, f32[16,256,256]{2,1,0:T(8,128)S(1)}, f32[16,256,128]{2,1,0:T(8,128)S(1)}, bf16[256,2048]{1,0:T(8,128)(2,1)S(1)},...) custom-call(bf16[32,512]{1,0:T(8,128)(2,1)} %latent.1, ...), custom_call_target="tpu_custom_call" | custom-call | flops 4000000000 | bytes 8000000 | tf_op jit(solution)/shard_map/pallas_call | solution.py:450
  29.3 5.6 %shard_map.132 = (bf16[256,2048]{1,0:T(8,128)(2,1)}, f32[1,512]{1,0:T(1,128)}) custom-call(f32[8,128]{1,0:T(8,128)S(1)} %get-tuple-element.16.seen, f32[16,256,256]{2,1,0:T(8,128)S(1)} %get-tuple-element.17.own_out, f32[16,256,128]{2,1,0:T(8,128)S(1)} %get-tuple-element.18.own_top, bf16[256,2048]{1,0:T(8,128)(2,1)S(1)} %get-tuple-element.19.qn, ...), custom_call_target="tpu_custom_call" | custom-call | flops 10000000000 | bytes 8000000 | tf_op jit(solution)/shard_map/pallas_call | solution.py:501

commit v4 on v3

--- a/solution.py
+++ b/solution.py
@@ -40,10 +40,10 @@
 def kernel(
     n_ctx, n_head, gain,
     latent, prior, k_rope, seg, q_nope, q_rope, w_uk, w_uv, q_cos, q_sin, k_cos, k_sin,
-    seen, own_out, own_top, qn, qx, kt, kx, vals, oldest, uk, uv, amax_out,
+    seen, own_out, own_top, qn, qx, kt, kx, vals, earlier_two, uk, uv, amax_out,
     lat, tops, z_tops, prior_v, seg_v, qr, qc, qs, kc, ks, clipped, kt3, vals3,
     own_recv, own_send, pair_recv, pair_send, side_recv, side_send, far_recv, far_send,
-    sib_send, sib_recv, tops_recv, tops_send, z_recv, z_send, load,
+    sib_send, sib_recv, tops_recv, tops_send, z_recv, z_send, hello, load,
 ):
     ctx = lax.axis_index("ctx")
     me = lax.axis_index("head")
@@ -100,14 +100,13 @@
     @pl.when((core == 0) & has0)
     def _():
         greet(ctx - 3, me)
-        greet(ctx - 3, beside)
 
     for k in range(1, n_head):
         greet(ctx, lax.rem(me + k, n_head))
     for d in (1, 2, 3):
         greet(4 * z + lax.rem(kind + d, 4), me)
     for k in range(1, n_z):
-        greet(4 * lax.rem(z + k, n_z) + kind, me)
+        pl.when(z + k < n_z)(functools.partial(greet, ctx + 4 * k, me))
 
     for slot, there in ((0, has0), (1, has1), (2, has2)):
         @pl.when(jnp.logical_not(there))
@@ -120,8 +119,8 @@
     lat[3, pl.ds(tokens + half, 16), :] = jnp.broadcast_to(
         jnp.concatenate([seg_v[...], seg_v[...]], axis=1).astype(F32), (16, width)
     ).astype(BF16)
-    listeners = 2 * (next2.astype(jnp.int32) + next3.astype(jnp.int32))
-    pl.semaphore_wait(barrier, n_head - 1 + 3 + (n_z - 1) + listeners)
+    listeners = 2 * next2.astype(jnp.int32) + next3.astype(jnp.int32)
+    pl.semaphore_wait(barrier, n_head - 1 + 3 + z + listeners)
 
     def share(k):
         return remote(
@@ -135,7 +134,7 @@
         return remote(lat.at[3, key_rows], lat.at[slot, key_rows], pair_send.at[slot, 2], pair_recv.at[slot, 2], c, me)
 
     ahead2 = [chunk(1, 0, ctx + 2, me), chunk(1, 1, ctx + 2, beside), keys_to(1, ctx + 2)]
-    ahead3 = [chunk(0, 0, ctx + 3, me), chunk(0, 1, ctx + 3, beside), keys_to(0, ctx + 3)]
+    ahead3 = remote(lat.at[3], lat.at[0], sib_send.at[2], sib_recv.at[0], ctx + 3, me)
 
     @pl.when(next2)
     def _():
@@ -145,13 +144,13 @@
     for k in range(1, n_head):
         share(k).start()
 
-    @pl.when(next3)
-    def _():
-        for copy in ahead3:
-            copy.start()
-
     for copy in loading[10:]:
         copy.start()
+
+    for k in range(1, n_z):
+        @pl.when(z - k >= 0)
+        def _(k=k):
+            pl.semaphore_signal(hello, inc=1, device_id=(ctx - 4 * k, me), device_id_type=MESH)
 
     for copy in loading[4:10]:
         copy.wait()
@@ -207,29 +206,23 @@
             side(slots, i, up).wait_send()
             far(slots, i, up, up).wait_send()
 
-    with_oldest = (core == 0) & has0
-    without_oldest = has1 & jnp.logical_not(with_oldest)
+    late = pl.ds(1, 1)
 
     def earlier(act):
-        pl.when(with_oldest)(functools.partial(act, pl.ds(0, 2)))
-        pl.when(without_oldest)(functools.partial(act, pl.ds(1, 1)))
+        pl.when(has1)(functools.partial(act, late))
 
     @pl.when(has1)
     def _():
         for copy in ahead2:
             copy.wait_recv()
 
-    @pl.when(with_oldest)
-    def _():
-        for copy in ahead3:
-            copy.wait_recv()
-
     earlier(sides)
 
     others = lat.at[3, pl.ds(0, (n_head - 1) * rows)]
     remote(others, others, own_send, own_recv, ctx, me).wait_recv()
     pass_own = remote(lat.at[3], lat.at[2], sib_send.at[0], sib_recv.at[2], sibling, me)
     pl.when(core == 0)(pass_own.start)
+    pl.when(next3)(ahead3.start)
     tops[kind] = jnp.max(jnp.abs(lat[3, block, :].astype(F32)), axis=0, keepdims=True)
 
     def spread_top(d):
@@ -243,24 +236,18 @@
         copy.wait()
 
     def project(slot):
-        at = pl.ds((slot - 1) * tokens, tokens)
+        kt_to, vals_to = (kt3, vals3) if slot == 3 else (kt, vals)
         clipped[...] = jnp.clip(lat[slot, block, :], -limit, limit)
 
         def some(g, carry):
             c = clipped[...]
             ups = (nt(uk[pl.ds(4 * g, 4)].reshape(4 * hd, width), c) * gain).astype(BF16).reshape(4, hd, tokens)
-            if slot == 3:
-                kt3[pl.ds(4 * g, 4)] = ups
-            else:
-                kt[pl.ds(4 * g, 4), :, at] = ups
+            kt_to[pl.ds(4 * g, 4)] = ups
             for p in range(2):
                 h = 4 * g + 2 * p
                 both = nn(c, jnp.concatenate([uv[h], uv[h + 1]], axis=1)).astype(BF16)
                 for e in range(2):
-                    if slot == 3:
-                        vals3[h + e] = both[:, e * hd:(e + 1) * hd]
-                    else:
-                        vals[h + e, at, :] = both[:, e * hd:(e + 1) * hd]
+                    vals_to[h + e] = both[:, e * hd:(e + 1) * hd]
             return carry
 
         lax.fori_loop(0, heads // 4, some, 0)
@@ -280,6 +267,18 @@
         kx[1, 64:128, at] = turned
 
     project(3)
+
+    three = tops.at[pl.ds(0, 3)]
+    remote(three, three, tops_send, tops_recv, ctx, me).wait_recv()
+    z_tops[z] = jnp.max(tops[...], axis=0)
+    pl.when(z < n_z - 1)(lambda: pl.semaphore_wait(hello, n_z - 1 - z))
+
+    def spread_z(k):
+        return remote(z_tops.at[z], z_tops.at[z], z_send, z_recv, 4 * lax.rem(z + k, n_z) + kind, me)
+
+    for k in range(1, n_z):
+        spread_z(k).start()
+
     turn_keys(3)
     earlier(fars)
 
@@ -298,16 +297,6 @@
 
     attend_own(0)
 
-    three = tops.at[pl.ds(0, 3)]
-    remote(three, three, tops_send, tops_recv, ctx, me).wait_recv()
-    z_tops[z] = jnp.max(tops[...], axis=0)
-
-    def spread_z(k):
-        return remote(z_tops.at[z], z_tops.at[z], z_send, z_recv, 4 * lax.rem(z + k, n_z) + kind, me)
-
-    for k in range(1, n_z):
-        spread_z(k).start()
-
     earlier(complete)
     on = [
         ((core == 0) & has1, remote(lat.at[1], lat.at[0], sib_send.at[1], sib_recv.at[0], sibling, me)),
@@ -317,15 +306,15 @@
         pl.when(there)(copy.start)
 
     attend_own(heads // 2)
-    project(1)
+    earlier_two[1] = jnp.clip(lat[1, block, :], -limit, limit)
     turn_keys(1)
 
     pl.when(has2)(pass_own.wait_recv)
     project(2)
     turn_keys(2)
 
-    pl.when((core == 1) & has0)(on[0][1].wait_recv)
-    oldest[...] = jnp.clip(lat[0, block, :], -limit, limit)
+    pl.when(has0)(ahead3.wait_recv)
+    earlier_two[0] = jnp.clip(lat[0, block, :], -limit, limit)
     turn_keys(0)
 
     doc_at = pl.ds(tokens + half, 16)
@@ -333,7 +322,8 @@
     count = jnp.zeros((1, 1), F32)
     for slot in range(3):
         count += (lat[slot, doc_at, 0:tokens].astype(F32)[0:1, tokens - 1:] == doc).astype(F32)
-    seen[...] = jnp.broadcast_to(count, seen.shape)
+    wide = (lat[3, doc_at, 0:tokens].astype(F32)[0:1, tokens // 2:tokens // 2 + 1] == doc).astype(F32)
+    seen[...] = jnp.broadcast_to(count + 4.0 * wide, seen.shape)
 
     rest = z_tops.at[pl.ds(0, n_z - 1)]
     remote(rest, rest, z_send, z_recv, ctx, me).wait_recv()
@@ -349,78 +339,83 @@
         for copy in ahead2:
             copy.wait_send()
 
-    @pl.when(next3)
-    def _():
-        for copy in ahead3:
-            copy.wait_send()
-
+    pl.when(next3)(ahead3.wait_send)
     pl.when(core == 0)(pass_own.wait_send)
     pl.when(has1)(on[0][1].wait_send)
 
 
 def attend(
-    gain, seen, own_out, own_top, qn, qx, kt, kx, vals, oldest, uk, uv, amax,
-    out, amax_out, kt0, vals0, outs, store, amax_store,
+    gain, seen, own_out, own_top, qn, qx, kt, kx, vals, earlier_two, uk, uv, amax,
+    out, amax_out, kt_two, vals_two, outs, store, amax_store,
 ):
     heads, hd, width = uk.shape
     tokens = qn.shape[0]
     write_amax = pltpu.make_async_copy(amax, amax_out, amax_store)
     write_amax.start()
-    count = jnp.max(seen[...]).astype(jnp.int32)
+    code = jnp.max(seen[...]).astype(jnp.int32)
+    count = code & 3
+    middle = tokens // 2
     together = min(heads, 8)
 
     def write(p):
         some = pl.ds(pl.multiple_of(p * 4 * hd, 4 * hd), 4 * hd)
         return pltpu.make_async_copy(outs.at[:, some], out.at[:, some], store.at[p])
 
-    @pl.when(count == 3)
-    def _():
-        def some(g, carry):
-            c = oldest[...]
-            ups = nt(uk[pl.ds(4 * g, 4)].reshape(4 * hd, width), c) * gain
-            kt0[pl.ds(4 * g, 4)] = ups.astype(BF16).reshape(4, hd, tokens)
-            for p in range(2):
-                h = 4 * g + 2 * p
-                both = nn(c, jnp.concatenate([uv[h], uv[h + 1]], axis=1)).astype(BF16)
-                vals0[h] = both[:, :hd]
-                vals0[h + 1] = both[:, hd:]
-            return carry
-
-        lax.fori_loop(0, heads // 4, some, 0)
-
-    def with_blocks(blocks):
+    for slot in range(2):
+        @pl.when(count >= 3 - slot)
+        def _(slot=slot):
+            def some(g, carry):
+                c = earlier_two[slot]
+                ups = nt(uk[pl.ds(4 * g, 4)].reshape(4 * hd, width), c) * gain
+                kt_two[slot, pl.ds(4 * g, 4)] = ups.astype(BF16).reshape(4, hd, tokens)
+                for p in range(2):
+                    h = 4 * g + 2 * p
+                    both = nn(c, jnp.concatenate([uv[h], uv[h + 1]], axis=1)).astype(BF16)
+                    vals_two[slot, h] = both[:, :hd]
+                    vals_two[slot, h + 1] = both[:, hd:]
+                return carry
+
+            lax.fori_loop(0, heads // 4, some, 0)
+
+    def with_blocks(blocks, wide):
+        seeing = 0 if not blocks else tokens if wide else middle
+        skip = middle if wide and blocks == 3 else 0
+
         def group(g, carry):
             for i in range(together):
                 h = together * g + i
                 e = i % 2
                 cols = pl.ds(pl.multiple_of(h * hd, hd), hd)
-                o = own_out[h]
                 if blocks:
-                    q = jnp.concatenate([qn[:, cols], qx[h]], axis=1)
-                    if blocks == 3:
-                        k = jnp.concatenate([kt0[h], kt[h]], axis=1)
-                        v = jnp.concatenate([vals0[h], vals[h]], axis=0)
-                    else:
-                        k = kt[h, :, (2 - blocks) * tokens:]
-                        v = vals[h, (2 - blocks) * tokens:, :]
-                    k = jnp.concatenate([k, kx[e, :, (3 - blocks) * tokens:3 * tokens]], axis=0)
+                    q = jnp.concatenate([qn[0:seeing, cols], qx[h, 0:seeing, :]], axis=1)
+                    k = [kt_two[x, h] for x in range(3 - blocks, 2)] + [kt[h]]
+                    v = [vals_two[x, h] for x in range(3 - blocks, 2)] + [vals[h]]
+                    k[0], v[0] = k[0][:, skip:], v[0][skip:]
+                    k = jnp.concatenate(k, axis=1)
+                    v = jnp.concatenate(v, axis=0)
+                    k = jnp.concatenate([k, kx[e, :, (3 - blocks) * tokens + skip:3 * tokens]], axis=0)
                     s = nn(q, k)
-                    own = own_top[h]
-                    top = jnp.maximum(jnp.max(s, axis=1, keepdims=True), own[:, 0:1])
-                    w = jnp.exp2(s - top).astype(BF16)
+                    own = own_top[h, 0:seeing, :]
+                    top = jnp.maximum(jnp.broadcast_to(jnp.max(s, axis=1, keepdims=True), own.shape), own)
+                    w = jnp.exp2(s - jnp.concatenate([top] * (s.shape[1] // hd), axis=1)).astype(BF16)
                     scale = jnp.exp2(own - top)
-                    o = o * jnp.concatenate([scale, scale], axis=1) + nn(
-                        w, jnp.concatenate([v, jnp.ones((blocks * tokens, hd), BF16)], axis=1)
+                    o = own_out[h, 0:seeing, :] * jnp.concatenate([scale, scale], axis=1) + nn(
+                        w, jnp.concatenate([v, jnp.ones(v.shape, BF16)], axis=1)
                     )
-                outs[:, cols] = (o[:, :hd] / o[:, hd:]).astype(BF16)
+                    outs[0:seeing, cols] = (o[:, :hd] / o[:, hd:]).astype(BF16)
+                if seeing < tokens:
+                    o = own_out[h, seeing:, :]
+                    outs[seeing:, cols] = (o[:, :hd] / o[:, hd:]).astype(BF16)
                 if i % 4 == 3:
                     write(together // 4 * g + i // 4).start()
             return carry
 
         lax.fori_loop(0, heads // together, group, 0)
 
-    for blocks in range(4):
-        pl.when(count == blocks)(functools.partial(with_blocks, blocks))
+    pl.when(count == 0)(functools.partial(with_blocks, 0, False))
+    for blocks in range(1, 4):
+        for wide in (False, True):
+            pl.when(code == blocks + 4 * wide)(functools.partial(with_blocks, blocks, wide))
 
     def written(p, carry):
         write(p).wait()
@@ -455,10 +450,10 @@
             pltpu.VMEM((heads, tokens, hd), F32),
             pltpu.VMEM((tokens, columns), BF16),
             pltpu.VMEM((heads, tokens, 128), BF16),
-            pltpu.VMEM((heads, hd, 2 * tokens), BF16),
+            pltpu.VMEM((heads, hd, tokens), BF16),
             pltpu.VMEM((2, 128, keys), BF16),
-            pltpu.VMEM((heads, 2 * tokens, hd), BF16),
-            pltpu.VMEM((tokens, width), BF16),
+            pltpu.VMEM((heads, tokens, hd), BF16),
+            pltpu.VMEM((2, tokens, width), BF16),
             pltpu.VMEM((heads, hd, width), BF16),
             pltpu.VMEM((heads, width, hd), BF16),
             pltpu.VMEM((1, width), F32),
@@ -487,12 +482,13 @@
             dma((2,)),
             dma((2,)),
             dma((2,)),
-            dma((2,)),
+            dma((3,)),
             dma((BLOCKS,)),
             dma,
             dma,
             dma,
             dma,
+            pltpu.SemaphoreType.REGULAR,
             dma((13,)),
         ],
         compiler_params=pltpu.CompilerParams(collective_id=0, has_side_effects=True, vmem_limit_bytes=18 * mib),
@@ -504,8 +500,8 @@
         in_specs=[in_vmem] * 12,
         out_specs=(anywhere, anywhere),
         scratch_shapes=[
-            pltpu.VMEM((heads, hd, tokens), BF16),
-            pltpu.VMEM((heads, tokens, hd), BF16),
+            pltpu.VMEM((2, heads, hd, tokens), BF16),
+            pltpu.VMEM((2, heads, tokens, hd), BF16),
             pltpu.VMEM((tokens, columns), BF16),
             dma((heads // 4,)),
             dma,

time: 34.9 us -> 29.8 us (0.85)
  the two profiles are of different devices: /device:TPU:32 before, /device:TPU:6 now
where the time goes in v4:
time: 29.8 us; the launch traced here: 29.7 us
  Pallas kernels  29 us (97%)
  between operations  0.64 us (2%)
    pallas_call x1, Pallas kernels, shards(): pl.pallas_call(functools.partial(kernel, n_ctx, n_head, gain), out_shape=...  24.1 us
    pallas_call x1, Pallas kernels, shards(): pl.pallas_call(functools.partial(attend, gain), out_shape=(jax.ShapeDtype...  4.93 us

profile of v4, /device:TPU:6, one launch (start us, length us, event | category | flops | bytes accessed | tf_op | source)
XLA Modules:
  0.0 29.7 jit_solution(13039191543274772474)
XLA Ops:
  0.6 24.1 %shard_map.131 = (f32[8,128]{1,0:T(8,128)S(1)}, f32[16,256,256]{2,1,0:T(8,128)S(1)}, f32[16,256,128]{2,1,0:T(8,128)S(1)}, bf16[256,2048]{1,0:T(8,128)(2,1)S(1)},...) custom-call(bf16[32,512]{1,0:T(8,128)(2,1)} %latent.1, ...), custom_call_target="tpu_custom_call" | custom-call | flops 4000000000 | bytes 8000000 | tf_op jit(solution)/shard_map/pallas_call | solution.py:445
  24.7 4.9 %shard_map.132 = (bf16[256,2048]{1,0:T(8,128)(2,1)}, f32[1,512]{1,0:T(1,128)}) custom-call(f32[8,128]{1,0:T(8,128)S(1)} %get-tuple-element.16.seen, f32[16,256,256]{2,1,0:T(8,128)S(1)} %get-tuple-element.17.own_out, f32[16,256,128]{2,1,0:T(8,128)S(1)} %get-tuple-element.18.own_top, bf16[256,2048]{1,0:T(8,128)(2,1)S(1)} %get-tuple-element.19.qn, ...), custom_call_target="tpu_custom_call" | custom-call | flops 10000000000 | bytes 8000000 | tf_op jit(solution)/shard_map/pallas_call | solution.py:497

commit v5 on v4

--- a/solution.py
+++ b/solution.py
@@ -171,7 +171,7 @@
         qx[2 * p + 1] = jnp.where(lane < 64, mark, turned).astype(BF16)
         return carry
 
-    lax.fori_loop(0, heads // 2, turn, 0, unroll=2)
+    lax.fori_loop(0, heads // 2, turn, 0, unroll=True)
 
     def pair_at(h):
         return pl.ds(pl.multiple_of(h // 2 * 2 * rows, 2 * rows), 2 * rows)
@@ -230,6 +230,8 @@
 
     for d in (1, 2, 3):
         spread_top(d).start()
+
+    earlier(fars)
 
     limit = prior_v[...].astype(BF16)
     for copy in loading[10:]:
@@ -250,7 +252,7 @@
                     vals_to[h + e] = both[:, e * hd:(e + 1) * hd]
             return carry
 
-        lax.fori_loop(0, heads // 4, some, 0)
+        lax.fori_loop(0, heads // 4, some, 0, unroll=True)
 
     def turn_keys(slot):
         at = pl.ds(slot * tokens, tokens)
@@ -280,7 +282,14 @@
         spread_z(k).start()
 
     turn_keys(3)
-    earlier(fars)
+
+    earlier(complete)
+    on = [
+        ((core == 0) & has1, remote(lat.at[1], lat.at[0], sib_send.at[1], sib_recv.at[0], sibling, me)),
+        ((core == 1) & has1, remote(lat.at[1], lat.at[2], sib_send.at[1], sib_recv.at[2], sibling, me)),
+    ]
+    for there, copy in on:
+        pl.when(there)(copy.start)
 
     q_at = lax.broadcasted_iota(jnp.int32, (tokens, tokens), 0)
     k_at = lax.broadcasted_iota(jnp.int32, (tokens, tokens), 1)
@@ -296,16 +305,8 @@
             own_top[h] = jnp.broadcast_to(top, (tokens, hd))
 
     attend_own(0)
-
-    earlier(complete)
-    on = [
-        ((core == 0) & has1, remote(lat.at[1], lat.at[0], sib_send.at[1], sib_recv.at[0], sibling, me)),
-        ((core == 1) & has1, remote(lat.at[1], lat.at[2], sib_send.at[1], sib_recv.at[2], sibling, me)),
-    ]
-    for there, copy in on:
-        pl.when(there)(copy.start)
-
     attend_own(heads // 2)
+
     earlier_two[1] = jnp.clip(lat[1, block, :], -limit, limit)
     turn_keys(1)
 
@@ -375,7 +376,7 @@
                     vals_two[slot, h + 1] = both[:, hd:]
                 return carry
 
-            lax.fori_loop(0, heads // 4, some, 0)
+            lax.fori_loop(0, heads // 4, some, 0, unroll=True)
 
     def with_blocks(blocks, wide):
         seeing = 0 if not blocks else tokens if wide else middle

time: 29.8 us -> 30.1 us (1.010)
  the two profiles are of different devices: /device:TPU:6 before, /device:TPU:7 now
where the time goes in v5:
time: 30.1 us
  Pallas kernels  29.2 us (97%)
  between operations  0.8 us (3%)
    pallas_call x1, Pallas kernels, shards(): pl.pallas_call(functools.partial(kernel, n_ctx, n_head, gain), out_shape=...  23.5 us
    pallas_call x1, Pallas kernels, shards(): pl.pallas_call(functools.partial(attend, gain), out_shape=(jax.ShapeDtype...  5.72 us

profile of v5, /device:TPU:7, one launch (start us, length us, event | category | flops | bytes accessed | tf_op | source)
XLA Modules:
  0.0 30.1 jit_solution(17457751977124520431)
XLA Ops:
  0.6 23.5 %shard_map.131 = (f32[8,128]{1,0:T(8,128)S(1)}, f32[16,256,256]{2,1,0:T(8,128)S(1)}, f32[16,256,128]{2,1,0:T(8,128)S(1)}, bf16[256,2048]{1,0:T(8,128)(2,1)S(1)},...) custom-call(bf16[32,512]{1,0:T(8,128)(2,1)} %latent.1, ...), custom_call_target="tpu_custom_call" | custom-call | flops 4000000000 | bytes 8000000 | tf_op jit(solution)/shard_map/pallas_call | solution.py:446
  24.2 5.7 %shard_map.132 = (bf16[256,2048]{1,0:T(8,128)(2,1)}, f32[1,512]{1,0:T(1,128)}) custom-call(f32[8,128]{1,0:T(8,128)S(1)} %get-tuple-element.16.seen, f32[16,256,256]{2,1,0:T(8,128)S(1)} %get-tuple-element.17.own_out, f32[16,256,128]{2,1,0:T(8,128)S(1)} %get-tuple-element.18.own_top, bf16[256,2048]{1,0:T(8,128)(2,1)S(1)} %get-tuple-element.19.qn, ...), custom_call_target="tpu_custom_call" | custom-call | flops 10000000000 | bytes 8000000 | tf_op jit(solution)/shard_map/pallas_call | solution.py:498

commit v6 on v5

--- a/solution.py
+++ b/solution.py
@@ -136,14 +136,14 @@
     ahead2 = [chunk(1, 0, ctx + 2, me), chunk(1, 1, ctx + 2, beside), keys_to(1, ctx + 2)]
     ahead3 = remote(lat.at[3], lat.at[0], sib_send.at[2], sib_recv.at[0], ctx + 3, me)
 
+    for k in range(1, n_head):
+        share(k).start()
+
     @pl.when(next2)
     def _():
         for copy in ahead2:
             copy.start()
 
-    for k in range(1, n_head):
-        share(k).start()
-
     for copy in loading[10:]:
         copy.start()
 
@@ -151,6 +151,64 @@
         @pl.when(z - k >= 0)
         def _(k=k):
             pl.semaphore_signal(hello, inc=1, device_id=(ctx - 4 * k, me), device_id_type=MESH)
+
+    def pair_at(h):
+        return pl.ds(pl.multiple_of(h // 2 * 2 * rows, 2 * rows), 2 * rows)
+
+    def one_at(h, x):
+        return pl.ds(pl.multiple_of((h // 2 * 2 + x) * rows, rows), rows)
+
+    def side(slots, i, to):
+        at = lat.at[slots, pair_at(me)]
+        return remote(at, at, side_send.at[i], side_recv.at[i], ctx, to)
+
+    def far(slots, i, h, to):
+        at = lat.at[slots, one_at(h, i)]
+        return remote(at, at, far_send.at[i], far_recv.at[i], ctx, to)
+
+    def sides(slots):
+        side(slots, 0, up).start()
+        side(slots, 1, down).start()
+
+    def fars(slots):
+        side(slots, 0, up).wait_recv()
+        far(slots, 0, down, up).start()
+        side(slots, 1, down).wait_recv()
+        far(slots, 1, up, down).start()
+
+    def complete(slots):
+        far(slots, 0, down, up).wait_recv()
+        far(slots, 1, up, down).wait_recv()
+
+    def sent(slots):
+        for i in range(2):
+            side(slots, i, up).wait_send()
+            far(slots, i, up, up).wait_send()
+
+    late = pl.ds(1, 1)
+
+    def earlier(act):
+        pl.when(has1)(functools.partial(act, late))
+
+    @pl.when(has1)
+    def _():
+        for copy in ahead2:
+            copy.wait_recv()
+
+    earlier(sides)
+
+    others = lat.at[3, pl.ds(0, (n_head - 1) * rows)]
+    remote(others, others, own_send, own_recv, ctx, me).wait_recv()
+    pass_own = remote(lat.at[3], lat.at[2], sib_send.at[0], sib_recv.at[2], sibling, me)
+    pl.when(core == 0)(pass_own.start)
+    pl.when(next3)(ahead3.start)
+    tops[kind] = jnp.max(jnp.abs(lat[3, block, :].astype(F32)), axis=0, keepdims=True)
+
+    def spread_top(d):
+        return remote(tops.at[kind], tops.at[kind], tops_send, tops_recv, 4 * z + lax.rem(kind + d, 4), me)
+
+    for d in (1, 2, 3):
+        spread_top(d).start()
 
     for copy in loading[4:10]:
         copy.wait()
@@ -173,65 +231,17 @@
 
     lax.fori_loop(0, heads // 2, turn, 0, unroll=True)
 
-    def pair_at(h):
-        return pl.ds(pl.multiple_of(h // 2 * 2 * rows, 2 * rows), 2 * rows)
-
-    def one_at(h, x):
-        return pl.ds(pl.multiple_of((h // 2 * 2 + x) * rows, rows), rows)
-
-    def side(slots, i, to):
-        at = lat.at[slots, pair_at(me)]
-        return remote(at, at, side_send.at[i], side_recv.at[i], ctx, to)
-
-    def far(slots, i, h, to):
-        at = lat.at[slots, one_at(h, i)]
-        return remote(at, at, far_send.at[i], far_recv.at[i], ctx, to)
-
-    def sides(slots):
-        side(slots, 0, up).start()
-        side(slots, 1, down).start()
-
-    def fars(slots):
-        side(slots, 0, up).wait_recv()
-        far(slots, 0, down, up).start()
-        side(slots, 1, down).wait_recv()
-        far(slots, 1, up, down).start()
-
-    def complete(slots):
-        far(slots, 0, down, up).wait_recv()
-        far(slots, 1, up, down).wait_recv()
-
-    def sent(slots):
-        for i in range(2):
-            side(slots, i, up).wait_send()
-            far(slots, i, up, up).wait_send()
-
-    late = pl.ds(1, 1)
-
-    def earlier(act):
-        pl.when(has1)(functools.partial(act, late))
-
-    @pl.when(has1)
-    def _():
-        for copy in ahead2:
-            copy.wait_recv()
-
-    earlier(sides)
-
-    others = lat.at[3, pl.ds(0, (n_head - 1) * rows)]
-    remote(others, others, own_send, own_recv, ctx, me).wait_recv()
-    pass_own = remote(lat.at[3], lat.at[2], sib_send.at[0], sib_recv.at[2], sibling, me)
-    pl.when(core == 0)(pass_own.start)
-    pl.when(next3)(ahead3.start)
-    tops[kind] = jnp.max(jnp.abs(lat[3, block, :].astype(F32)), axis=0, keepdims=True)
-
-    def spread_top(d):
-        return remote(tops.at[kind], tops.at[kind], tops_send, tops_recv, 4 * z + lax.rem(kind + d, 4), me)
-
-    for d in (1, 2, 3):
-        spread_top(d).start()
-
     earlier(fars)
+
+    three = tops.at[pl.ds(0, 3)]
+    remote(three, three, tops_send, tops_recv, ctx, me).wait_recv()
+    z_tops[z] = jnp.max(tops[...], axis=0)
+
+    def spread_z(k):
+        return remote(z_tops.at[z], z_tops.at[z], z_send.at[k + n_z], z_recv, ctx + 4 * k, me)
+
+    for k in range(1, n_z):
+        pl.when(z - k >= 0)(spread_z(-k).start)
 
     limit = prior_v[...].astype(BF16)
     for copy in loading[10:]:
@@ -270,17 +280,6 @@
 
     project(3)
 
-    three = tops.at[pl.ds(0, 3)]
-    remote(three, three, tops_send, tops_recv, ctx, me).wait_recv()
-    z_tops[z] = jnp.max(tops[...], axis=0)
-    pl.when(z < n_z - 1)(lambda: pl.semaphore_wait(hello, n_z - 1 - z))
-
-    def spread_z(k):
-        return remote(z_tops.at[z], z_tops.at[z], z_send, z_recv, 4 * lax.rem(z + k, n_z) + kind, me)
-
-    for k in range(1, n_z):
-        spread_z(k).start()
-
     turn_keys(3)
 
     earlier(complete)
@@ -305,6 +304,13 @@
             own_top[h] = jnp.broadcast_to(top, (tokens, hd))
 
     attend_own(0)
+
+    @pl.when(z < n_z - 1)
+    def _():
+        pl.semaphore_wait(hello, n_z - 1 - z)
+        for k in range(1, n_z):
+            pl.when(z + k < n_z)(spread_z(k).start)
+
     attend_own(heads // 2)
 
     earlier_two[1] = jnp.clip(lat[1, block, :], -limit, limit)
@@ -327,12 +333,14 @@
     seen[...] = jnp.broadcast_to(count + 4.0 * wide, seen.shape)
 
     rest = z_tops.at[pl.ds(0, n_z - 1)]
-    remote(rest, rest, z_send, z_recv, ctx, me).wait_recv()
+    remote(rest, rest, z_send.at[0], z_recv, ctx, me).wait_recv()
     amax_out[...] = jnp.max(z_tops[...], axis=0)
 
     remote(others, others, own_send, own_recv, ctx, me).wait_send()
     remote(three, three, tops_send, tops_recv, ctx, me).wait_send()
-    remote(rest, rest, z_send, z_recv, ctx, me).wait_send()
+    for k in range(1, n_z):
+        pl.when(z - k >= 0)(spread_z(-k).wait_send)
+        pl.when(z + k < n_z)(spread_z(k).wait_send)
     earlier(sent)
 
     @pl.when(next2)
@@ -488,7 +496,7 @@
             dma,
             dma,
             dma,
-            dma,
+            dma((2 * n_z,)),
             pltpu.SemaphoreType.REGULAR,
             dma((13,)),
         ],

time: 30.1 us -> 30 us (level)
  the two profiles are of different devices: /device:TPU:7 before, /device:TPU:193 now
where the time goes in v6:
time: 30 us; the launch traced here: 29.9 us
  Pallas kernels  29.1 us (97%)
  between operations  0.8 us (3%)
    pallas_call x1, Pallas kernels, shards(): pl.pallas_call(functools.partial(kernel, n_ctx, n_head, gain), out_shape=...  20.5 us
    pallas_call x1, Pallas kernels, shards(): pl.pallas_call(functools.partial(attend, gain), out_shape=(jax.ShapeDtype...  8.57 us

profile of v6, /device:TPU:193, one launch (start us, length us, event | category | flops | bytes accessed | tf_op | source)
XLA Modules:
  0.0 29.9 jit_solution(16784085647657396156)
XLA Ops:
  0.6 20.5 %shard_map.131 = (f32[8,128]{1,0:T(8,128)S(1)}, f32[16,256,256]{2,1,0:T(8,128)S(1)}, f32[16,256,128]{2,1,0:T(8,128)S(1)}, bf16[256,2048]{1,0:T(8,128)(2,1)S(1)},...) custom-call(bf16[32,512]{1,0:T(8,128)(2,1)} %latent.1, ...), custom_call_target="tpu_custom_call" | custom-call | flops 4000000000 | bytes 8000000 | tf_op jit(solution)/shard_map/pallas_call | solution.py:454
  21.2 8.6 %shard_map.132 = (bf16[256,2048]{1,0:T(8,128)(2,1)}, f32[1,512]{1,0:T(1,128)}) custom-call(f32[8,128]{1,0:T(8,128)S(1)} %get-tuple-element.16.seen, f32[16,256,256]{2,1,0:T(8,128)S(1)} %get-tuple-element.17.own_out, f32[16,256,128]{2,1,0:T(8,128)S(1)} %get-tuple-element.18.own_top, bf16[256,2048]{1,0:T(8,128)(2,1)S(1)} %get-tuple-element.19.qn, ...), custom_call_target="tpu_custom_call" | custom-call | flops 10000000000 | bytes 8000000 | tf_op jit(solution)/shard_map/pallas_call | solution.py:506
